TPU v7x, 32 devices: a whole 2x2x4 slice. The times are simulated.
32 devices in a mesh: dp: 8 (over y, x, core), owner: 4 (over z).
Axes of the slice: x: 2, y: 2, z: 4, core: 2. Of those that a mesh axis runs over, the one named last changes fastest.
Arguments:
- inputs: bfloat16 [32, 1024, 1536], P(('dp', 'owner')), may hold values from -6 to 6
- cotangent: bfloat16 [32, 1024, 1536], P(('dp', 'owner')), may hold values from -6 to 6
- lengths: int32 [32], replicated, may hold values from 1 to 1024, 16384 in all
- balance: int32 [32], replicated, may hold values from 0 to 31, each once
- owner_slot_tile: int32 [1920], replicated, may hold values from 0 to 1919, as said below
- master: float32 [1920, 128, 128], P(('dp', 'owner'))
- first_moment: float32 [1920, 128, 128], P(('dp', 'owner'))
- second_moment: float32 [1920, 128, 128], P(('dp', 'owner')), as said below
- left_basis: float32 [1920, 128, 128], P(('dp', 'owner')), as said below
- right_basis: float32 [1920, 128, 128], P(('dp', 'owner')), as said below
- left_stat: float32 [1920, 128, 128], P(('dp', 'owner')), as said below
- right_stat: float32 [1920, 128, 128], P(('dp', 'owner')), as said below
- small_master: float32 [19456], P(('dp', 'owner'))
- small_first: float32 [19456], P(('dp', 'owner'))
- small_second: float32 [19456], P(('dp', 'owner')), as said below
Outputs:
- activation: bfloat16 [32, 1024, 1536], P(('dp', 'owner'))
- input_grad: bfloat16 [32, 1024, 1536], P(('dp', 'owner'))
- new_master: float32 [1920, 128, 128], P(('dp', 'owner'))
- new_first: float32 [1920, 128, 128], P(('dp', 'owner'))
- new_second: float32 [1920, 128, 128], P(('dp', 'owner'))
- new_left: float32 [1920, 128, 128], P(('dp', 'owner'))
- new_right: float32 [1920, 128, 128], P(('dp', 'owner'))
- new_left_stat: float32 [1920, 128, 128], P(('dp', 'owner'))
- new_right_stat: float32 [1920, 128, 128], P(('dp', 'owner'))
- small_new: float32 [19456], P(('dp', 'owner'))
- small_first_new: float32 [19456], P(('dp', 'owner'))
- small_second_new: float32 [19456], P(('dp', 'owner'))
Inputs may be any that keep to these rules, and one draw needn't show every extreme that they name: Each value once; slot s holds tile owner_slot_tile[s], values 1904 or more mark empty slots. `balance`: each sequence once. `lengths`: the longest sequence has exactly 1024 live positions. `left_basis`: each tile is orthogonal. `right_basis`: each tile is orthogonal. `left_stat`: each tile is symmetric with a positive, strictly dominant diagonal. `right_stat`: each tile is symmetric with a positive, strictly dominant diagonal. `second_moment`: positive. `small_second`: positive.
All inputs are finite; a program needn't handle non-finite values.
Results may differ from a plain program's by a relative error of at most 0.011.
The roundings to bfloat16 on the way count: a program that leaves them out, or rounds other values in their place, can miss the bound.
Values may be sent and summed in bfloat16 or wider, within the bound.
No kernel may reach another device: no remote copies, remote signals or barrier semaphores. Data moves between devices by JAX's collectives and lax.ppermute only.
A program may use at most 704 MiB of HBM per device.

v0:
```python
import jax
import jax.numpy as jnp
from jax import lax
from jax.sharding import PartitionSpec as P

D = 1536
R = 2048
F = 4608
KW = 4
STEP = 5
NT = 1904


EPS = 1e-06
BETA_ONE = 0.5
BETA_TWO = 0.6
BETA_STAT = 0.5
RATE = 0.02
SMALL_RATE = 0.6
DECAY = 0.01
ADAM_EPS = 1e-08
HIGH = lax.Precision.HIGHEST


def rms_norm(values, scales):
    return values * lax.rsqrt(jnp.mean(values * values, axis=-1, keepdims=True) + EPS) * scales


def causal_conv(values, kernel, shift_bias):
    length_now = values.shape[-2]
    total = shift_bias + kernel[0] * values
    for offset in range(1, kernel.shape[0]):
        padding = [(0, 0)] * (values.ndim - 2) + [(offset, 0), (0, 0)]
        total = total + kernel[offset] * jnp.pad(values, padding)[..., :length_now, :]
    return total


def lru_gates(rec_pre, inp_pre, conv_vals, rec_bias, inp_bias, decay_log):
    recall = jax.nn.sigmoid(rec_pre + rec_bias)
    admitted = jax.nn.sigmoid(inp_pre + inp_bias)
    log_keep = -8.0 * recall * jax.nn.softplus(-decay_log)
    return (jnp.exp(log_keep), jnp.sqrt(-jnp.expm1(2.0 * log_keep)) * admitted * conv_vals)


def combine(earlier, later):
    return (earlier[0] * later[0], later[0] * earlier[1] + later[1])


def mixgate(states, pre_vals):
    return states * jax.nn.gelu(pre_vals)


def gelu_gate(gate_vals, up_vals):
    return jax.nn.gelu(gate_vals) * up_vals


def untile(blocks, row_count, col_count):
    tile_edge = blocks.shape[-1]
    shaped = blocks.reshape(row_count // tile_edge, col_count // tile_edge, tile_edge, tile_edge)
    return shaped.transpose(0, 2, 1, 3).reshape(row_count, col_count)


def tiles_of(matrix, tile_edge):
    row_count, col_count = matrix.shape
    shaped = matrix.reshape(row_count // tile_edge, tile_edge, col_count // tile_edge, tile_edge)
    return shaped.transpose(0, 2, 1, 3).reshape(-1, tile_edge, tile_edge)


def split_tiles(tiles):
    tile_edge = tiles.shape[-1]
    across = D // tile_edge * (R // tile_edge)
    wide_count = D // tile_edge * (F // tile_edge)
    head_count = R // tile_edge
    mark_one = 3 * across
    mark_two = mark_one + 2 * head_count
    w_x = untile(tiles[0:across], D, R)
    w_y = untile(tiles[across : 2 * across], D, R)
    w_out = untile(tiles[2 * across : mark_one], R, D)
    w_rec = tiles[mark_one : mark_one + head_count]
    w_inp = tiles[mark_one + head_count : mark_two]
    w_gate = untile(tiles[mark_two : mark_two + wide_count], D, F)
    w_up = untile(tiles[mark_two + wide_count : mark_two + 2 * wide_count], D, F)
    w_down = untile(tiles[mark_two + 2 * wide_count : mark_two + 3 * wide_count], F, D)
    return (w_x, w_y, w_out, w_rec, w_inp, w_gate, w_up, w_down)


def split_small(vector):
    offset_base = 2 * D + KW * R
    gain_one = vector[0:D]
    gain_two = vector[D : 2 * D]
    conv_kernel = vector[2 * D : offset_base].reshape(KW, R)
    conv_bias = vector[offset_base : offset_base + R]
    rec_bias = vector[offset_base + R : offset_base + 2 * R]
    inp_bias = vector[offset_base + 2 * R : offset_base + 3 * R]
    decay_log = vector[offset_base + 3 * R : offset_base + 4 * R]
    return (gain_one, gain_two, conv_kernel, conv_bias, rec_bias, inp_bias, decay_log)


def orthonormal(matrix):
    gram_matrix = jnp.einsum("nki,nkj->nij", matrix, matrix, precision=HIGH)
    lower_factor = lax.linalg.cholesky(gram_matrix)
    return lax.linalg.triangular_solve(
        lower_factor, matrix, left_side=False, lower=True, transpose_a=True
    )


def rotate_step(
    grads, weights, first_vals, second_vals, left_vals, right_vals, left_stats, right_stats
):
    half_turn = jnp.einsum("nki,nkl->nil", left_vals, grads, precision=HIGH)
    turned = jnp.einsum("nil,nlj->nij", half_turn, right_vals, precision=HIGH)
    first_new = BETA_ONE * first_vals + (1.0 - BETA_ONE) * turned
    second_new = BETA_TWO * second_vals + (1.0 - BETA_TWO) * turned * turned
    scaled = (
        first_new
        / (1.0 - BETA_ONE**STEP)
        / (jnp.sqrt(second_new / (1.0 - BETA_TWO**STEP)) + ADAM_EPS)
    )
    back_half = jnp.einsum("nik,nkl->nil", left_vals, scaled, precision=HIGH)
    update = jnp.einsum("nil,njl->nij", back_half, right_vals, precision=HIGH)
    weight_new = weights - RATE * (update + DECAY * weights)
    left_stat_new = BETA_STAT * left_stats + (1.0 - BETA_STAT) * jnp.einsum(
        "nik,njk->nij", grads, grads, precision=HIGH
    )
    right_stat_new = BETA_STAT * right_stats + (1.0 - BETA_STAT) * jnp.einsum(
        "nki,nkj->nij", grads, grads, precision=HIGH
    )
    left_new = orthonormal(jnp.einsum("nik,nkj->nij", left_stat_new, left_vals, precision=HIGH))
    right_new = orthonormal(jnp.einsum("nik,nkj->nij", right_stat_new, right_vals, precision=HIGH))
    return (weight_new, first_new, second_new, left_new, right_new, left_stat_new, right_stat_new)


def small_step(grads, weights, first_vals, second_vals):
    first_new = BETA_ONE * first_vals + (1.0 - BETA_ONE) * grads
    second_new = BETA_TWO * second_vals + (1.0 - BETA_TWO) * grads * grads
    scaled = (
        first_new
        / (1.0 - BETA_ONE**STEP)
        / (jnp.sqrt(second_new / (1.0 - BETA_TWO**STEP)) + ADAM_EPS)
    )
    return (weights - SMALL_RATE * scaled, first_new, second_new)


def block_mul(values, blocks):
    head_count, tile_edge = (blocks.shape[0], blocks.shape[1])
    shaped = values.reshape(values.shape[:-1] + (head_count, tile_edge))
    product = jnp.einsum("...hi,hij->...hj", shaped, blocks, preferred_element_type=jnp.float32)
    return product.reshape(values.shape)


def block_back(grads, blocks):
    head_count, tile_edge = (blocks.shape[0], blocks.shape[1])
    shaped = grads.reshape(grads.shape[:-1] + (head_count, tile_edge))
    product = jnp.einsum("...hj,hij->...hi", shaped, blocks, preferred_element_type=jnp.float32)
    return product.reshape(grads.shape)


def block_grad(values, grads, blocks):
    head_count, tile_edge = (blocks.shape[0], blocks.shape[1])
    left_part = values.reshape(-1, head_count, tile_edge)
    right_part = grads.reshape(-1, head_count, tile_edge)
    return jnp.einsum("nhi,nhj->hij", left_part, right_part, preferred_element_type=jnp.float32)


def forward_mul(rows, weight):
    return jnp.dot(rows, weight, preferred_element_type=jnp.float32)


def row_product(left_rows, right_rows):
    return lax.dot_general(
        left_rows, right_rows, (((0,), (0,)), ((), ())), preferred_element_type=jnp.float32
    )


def back_product(rows, weight):
    return lax.dot_general(
        rows, weight, (((1,), (1,)), ((), ())), preferred_element_type=jnp.float32
    )


def permute_rows(selector, pieces):
    return jnp.einsum("jk,krd->jrd", selector, pieces, preferred_element_type=jnp.float32).astype(
        jnp.bfloat16
    )


def unpermute_rows(selector, pieces):
    return jnp.einsum("jk,jrd->krd", selector, pieces, preferred_element_type=jnp.float32).astype(
        jnp.bfloat16
    )


def body(
    inputs,
    cotangent,
    lengths,
    balance,
    owner_slot_tile,
    master,
    first_moment,
    second_moment,
    left_basis,
    right_basis,
    left_stat,
    right_stat,
    small_master,
    small_first,
    small_second,
):
    devices = lax.axis_size(("dp", "owner"))
    rank_now = lax.axis_index(("dp", "owner"))
    local_seqs, seq_len, width = inputs.shape
    total_seqs = local_seqs * devices
    slot_count = owner_slot_tile.shape[0]
    flat_rows = local_seqs * seq_len
    packed, small_packed = (
        lax.all_gather(master.astype(jnp.bfloat16), ("dp", "owner"), axis=0, tiled=True),
        lax.all_gather(small_master.astype(jnp.bfloat16), ("dp", "owner"), axis=0, tiled=True),
    )
    slot_lookup = (
        jnp.zeros((slot_count,), jnp.int32)
        .at[owner_slot_tile]
        .set(jnp.arange(slot_count, dtype=jnp.int32))
    )
    w_x, w_y, w_out, w_rec, w_inp, w_gate, w_up, w_down = split_tiles(packed[slot_lookup[:NT]])
    small_vals = small_packed.astype(jnp.float32)
    gain_one, gain_two, conv_kernel, conv_bias, rec_bias, inp_bias, decay_log = split_small(
        small_vals
    )
    selector = (balance[:, None] == jnp.arange(total_seqs, dtype=jnp.int32)[None, :]).astype(
        jnp.bfloat16
    )
    spread = lax.all_to_all(inputs, ("dp", "owner"), split_axis=1, concat_axis=0, tiled=True)
    tokens_in = lax.all_to_all(
        permute_rows(selector, spread), ("dp", "owner"), split_axis=0, concat_axis=1, tiled=True
    )
    my_slots = rank_now * local_seqs + jnp.arange(local_seqs, dtype=jnp.int32)
    my_lengths = lengths[balance[my_slots]]
    live_mask = (jnp.arange(seq_len, dtype=jnp.int32)[None, :] < my_lengths[:, None]).astype(
        jnp.float32
    )[:, :, None]
    tokens_f = tokens_in.astype(jnp.float32)
    normed_one, norm_one_back = jax.vjp(rms_norm, tokens_f, gain_one)
    normed_low = normed_one.astype(jnp.bfloat16).reshape(flat_rows, width)
    branch = forward_mul(normed_low, w_x).reshape(local_seqs, seq_len, R)
    gate_pre = forward_mul(normed_low, w_y).reshape(local_seqs, seq_len, R)
    conv_out, conv_pull = jax.vjp(causal_conv, branch, conv_kernel, conv_bias)
    conv_low = conv_out.astype(jnp.bfloat16)
    conv_f = conv_low.astype(jnp.float32)
    rec_pre = block_mul(conv_low, w_rec)
    inp_pre = block_mul(conv_low, w_inp)
    (decays, driven), gates_pull = jax.vjp(
        lru_gates, rec_pre, inp_pre, conv_f, rec_bias, inp_bias, decay_log
    )
    states = lax.associative_scan(combine, (decays, driven), axis=1)[1]
    mixed, mix_pull = jax.vjp(mixgate, states, gate_pre)
    mixed_low = mixed.astype(jnp.bfloat16).reshape(flat_rows, R)
    resid = tokens_f + forward_mul(mixed_low, w_out).reshape(local_seqs, seq_len, width)
    normed_two, norm_two_back = jax.vjp(rms_norm, resid, gain_two)
    normed_two_low = normed_two.astype(jnp.bfloat16).reshape(flat_rows, width)
    gate_act = forward_mul(normed_two_low, w_gate)
    up_act = forward_mul(normed_two_low, w_up)
    glu_out, glu_pull = jax.vjp(gelu_gate, gate_act, up_act)
    glu_low = glu_out.astype(jnp.bfloat16)
    result = resid + forward_mul(glu_low, w_down).reshape(local_seqs, seq_len, width)
    seq_back = cotangent.astype(jnp.float32) * live_mask
    down_back = seq_back.astype(jnp.bfloat16).reshape(flat_rows, width)
    grad_down = row_product(glu_low, down_back)
    glu_back = back_product(down_back, w_down)
    gate_back, up_back = glu_pull(glu_back)
    gate_back_low = gate_back.astype(jnp.bfloat16)
    up_back_low = up_back.astype(jnp.bfloat16)
    grad_gate = row_product(normed_two_low, gate_back_low)
    grad_up = row_product(normed_two_low, up_back_low)
    normed_two_back = (
        back_product(gate_back_low, w_gate) + back_product(up_back_low, w_up)
    ).reshape(local_seqs, seq_len, width)
    resid_norm_back, grad_gain_two = norm_two_back(normed_two_back)
    resid_back = seq_back + resid_norm_back
    out_back = resid_back.astype(jnp.bfloat16).reshape(flat_rows, width)
    grad_out = row_product(mixed_low, out_back)
    mixed_back = back_product(out_back, w_out).reshape(local_seqs, seq_len, R)
    states_back, pre_back = mix_pull(mixed_back)
    pre_back_low = pre_back.astype(jnp.bfloat16).reshape(flat_rows, R)
    edge_zeros = jnp.zeros((local_seqs, 1, R), jnp.float32)
    later_keep = jnp.concatenate([decays[:, 1:], edge_zeros], axis=1)
    carried = lax.associative_scan(combine, (later_keep, states_back), reverse=True, axis=1)[1]
    prior_states = jnp.concatenate([edge_zeros, states[:, :-1]], axis=1)
    rec_back, inp_back, conv_direct, grad_rec_bias, grad_inp_bias, grad_decay = gates_pull(
        (carried * prior_states, carried)
    )
    rec_back_low = rec_back.astype(jnp.bfloat16)
    inp_back_low = inp_back.astype(jnp.bfloat16)
    conv_back = conv_direct + block_back(rec_back_low, w_rec) + block_back(inp_back_low, w_inp)
    grad_rec = block_grad(conv_low, rec_back_low, w_rec)
    grad_inp = block_grad(conv_low, inp_back_low, w_inp)
    branch_back, grad_conv_kernel, grad_conv_bias = conv_pull(conv_back)
    branch_back_low = branch_back.astype(jnp.bfloat16).reshape(flat_rows, R)
    grad_x = row_product(normed_low, branch_back_low)
    grad_y = row_product(normed_low, pre_back_low)
    normed_one_back = (
        back_product(branch_back_low, w_x) + back_product(pre_back_low, w_y)
    ).reshape(local_seqs, seq_len, width)
    tokens_norm_back, grad_gain_one = norm_one_back(normed_one_back)
    tokens_back = resid_back + tokens_norm_back
    result_rows, grad_rows = (
        lax.all_to_all(
            result.astype(jnp.bfloat16), ("dp", "owner"), split_axis=1, concat_axis=0, tiled=True
        ),
        lax.all_to_all(
            tokens_back.astype(jnp.bfloat16),
            ("dp", "owner"),
            split_axis=1,
            concat_axis=0,
            tiled=True,
        ),
    )
    activation, input_grad = (
        lax.all_to_all(
            unpermute_rows(selector, result_rows),
            ("dp", "owner"),
            split_axis=0,
            concat_axis=1,
            tiled=True,
        ),
        lax.all_to_all(
            unpermute_rows(selector, grad_rows),
            ("dp", "owner"),
            split_axis=0,
            concat_axis=1,
            tiled=True,
        ),
    )
    tile_edge = master.shape[-1]
    grad_tiles = jnp.concatenate(
        [
            tiles_of(grad_x, tile_edge),
            tiles_of(grad_y, tile_edge),
            tiles_of(grad_out, tile_edge),
            grad_rec,
            grad_inp,
            tiles_of(grad_gate, tile_edge),
            tiles_of(grad_up, tile_edge),
            tiles_of(grad_down, tile_edge),
        ],
        axis=0,
    )
    filled = (owner_slot_tile < NT)[:, None, None]
    slot_grads = jnp.where(filled, grad_tiles[jnp.minimum(owner_slot_tile, NT - 1)], 0.0)
    small_grads = jnp.concatenate(
        [
            grad_gain_one,
            grad_gain_two,
            grad_conv_kernel.reshape(-1),
            grad_conv_bias,
            grad_rec_bias,
            grad_inp_bias,
            grad_decay,
        ],
        axis=0,
    )
    own_tiles, own_small = (
        lax.psum_scatter(slot_grads, ("dp", "owner"), scatter_dimension=0, tiled=True),
        lax.psum_scatter(small_grads, ("dp", "owner"), scatter_dimension=0, tiled=True),
    )
    new_master, new_first, new_second, new_left, new_right, new_left_stat, new_right_stat = (
        rotate_step(
            own_tiles,
            master,
            first_moment,
            second_moment,
            left_basis,
            right_basis,
            left_stat,
            right_stat,
        )
    )
    small_new, small_first_new, small_second_new = small_step(
        own_small, small_master, small_first, small_second
    )
    return (
        activation,
        input_grad,
        new_master,
        new_first,
        new_second,
        new_left,
        new_right,
        new_left_stat,
        new_right_stat,
        small_new,
        small_first_new,
        small_second_new,
    )


def solution(mesh):
    return jax.shard_map(
        body,
        mesh=mesh,
        in_specs=(
            P(("dp", "owner"), None, None),
            P(("dp", "owner"), None, None),
            P(),
            P(),
            P(),
            P(("dp", "owner"), None, None),
            P(("dp", "owner"), None, None),
            P(("dp", "owner"), None, None),
            P(("dp", "owner"), None, None),
            P(("dp", "owner"), None, None),
            P(("dp", "owner"), None, None),
            P(("dp", "owner"), None, None),
            P(("dp", "owner")),
            P(("dp", "owner")),
            P(("dp", "owner")),
        ),
        out_specs=(
            P(("dp", "owner"), None, None),
            P(("dp", "owner"), None, None),
            P(("dp", "owner"), None, None),
            P(("dp", "owner"), None, None),
            P(("dp", "owner"), None, None),
            P(("dp", "owner"), None, None),
            P(("dp", "owner"), None, None),
            P(("dp", "owner"), None, None),
            P(("dp", "owner"), None, None),
            P(("dp", "owner")),
            P(("dp", "owner")),
            P(("dp", "owner")),
        ),
        check_vma=False,
    )
```

profile of v0, /device:TPU:16, one launch (start us, length us, event | category | flops | bytes accessed | tf_op | source)
XLA Modules:
  0.0 6673.3 jit_solution(18344581311438083256)
XLA Ops:
  11.2 35.0 copy.427
  46.6 21.9 reduce.46
  75.8 147.5 %all_to_all.69 = bf16[32,2,24576]{2,1,0:T(2,128)(2,1)} all-to-all(bf16[32,2,24576]{2,1,0:T(2,128)(2,1)S(1)} %reshape.1039), channel_id=1, replica_groups=mesh['dp'=8,'owner'=4] {'dp','owner'}, dimensions={0} | all-to-all | bytes 6291456 | tf_op jit(solution)/shard_map/all_to_all | solution.py:233
  261.7 173.7 %all-reduce.52 = bf16[19456]{0:T(1024)(128)(2,1)S(1)} all-reduce(bf16[19456]{0:T(1024)(128)(2,1)S(1)} %dynamic-update-slice.3), channel_id=1, replica_groups=mesh['dp'=8,'owner'=4] {'dp','owner'}, use_global_device_ids=true, to_apply=%add.52 | all-reduce | flops 19456 | bytes 77824
  471.4 45.2 gather_fusion
  900.6 29.3 fusion.219
  1006.0 32.6 pad.193
  1038.5 32.5 pad.194
  1081.4 19.6 copy.252
  1146.4 37.2 copy.251
  1183.6 23.2 fusion.18
  1206.8 23.7 fusion.28
  1230.5 43.8 fusion.16
  1274.4 32.3 fusion.22
  1367.0 43.1 multiply_reduce_fusion.5
  1418.7 21.6 fusion.48
  1505.3 32.6 slice.678
  1537.9 32.6 slice.671
  1570.5 32.6 slice.675
  1603.2 32.8 slice.673
  1839.4 33.5 slice.747
  1873.0 33.7 slice.669
  1973.5 32.6 pad.213
  2006.2 32.5 pad.214
  2050.5 64.3 rev.2
  2114.8 22.5 multiply_reduce_fusion
  2178.2 27.7 fusion.214
  2372.5 22.0 fusion.246
  2394.5 20.4 fusion.247
  2434.1 24.0 constant_dynamic-update-slice_fusion.2
  2470.3 21.1 fusion.248
  2491.4 20.5 constant_dynamic-update-slice_fusion
  2511.9 85.0 %gather_fusion.1 = f32[1920,128,128]{2,1,0:T(8,128)} fusion(f32[1904,128,128]{2,1,0:T(8,128)} %constant_dynamic-update-slice_fusion, s32[2048]{0:T(1024)S(1)} %copy-done.85), kind=kCustom, calls=%fused_computation.1 | custom fusion | bytes 251665920 | tf_op jit(solution)/shard_map/gather | solution.py:349
  2596.9 80.9 %broadcast_select_fusion = f32[1920,128,128]{2,1,0:T(8,128)} fusion(f32[1920,128,128]{2,1,0:T(8,128)} %gather_fusion.1, pred[1920]{0:T(1024)(128)(4,1)S(1)} %copy-done.123), kind=kLoop, calls=%fused_computation.3 | loop fusion | flops 31457280 | bytes 251660160 | tf_op jit(solution)/shard_map/jit(_where)/select_n | solution.py:349
  2677.8 37.1 fusion.131
  2714.8 35.0 copy.426
  2749.8 22.1 reduce.47
  2807.7 35.0 copy.425
  2842.7 20.2 reduce.48
  2866.5 51.5 all-to-all-done.2
  2953.3 109.7 %all-to-all-done.4 = bf16[32,2,24576]{2,1,0:T(2,128)(2,1)S(1)} async-done(((bf16[32,2,24576]{2,1,0:T(2,128)(2,1)}), bf16[32,2,24576]{2,1,0:T(2,128)(2,1)S(1)}, u32[]{:S(2)}, u32[]{:S(2)}) %all-to-all-start.4) | async-done | bytes 3145760 | tf_op jit(solution)/shard_map/all_to_all | solution.py:310
  3099.7 108.6 %all-to-all-done.3 = bf16[32,32,1536]{2,1,0:T(8,128)(2,1)S(1)} async-done(((bf16[32,32,1536]{2,1,0:T(8,128)(2,1)}), bf16[32,32,1536]{2,1,0:T(8,128)(2,1)S(1)}, u32[]{:S(2)}, u32[]{:S(2)}) %all-to-all-start.3) | async-done | bytes 3145760 | tf_op jit(solution)/shard_map/all_to_all | solution.py:319
  3215.6 139.2 %all-to-all-done.5 = bf16[32,32,1536]{2,1,0:T(8,128)(2,1)} async-done(((bf16[32,32,1536]{2,1,0:T(8,128)(2,1)}), bf16[32,32,1536]{2,1,0:T(8,128)(2,1)}, u32[]{:S(2)}, u32[]{:S(2)}) %all-to-all-start.5) | async-done | bytes 3145760 | tf_op jit(solution)/shard_map/all_to_all | solution.py:326
  3354.8 552.6 %reduce-scatter.2.cloned.1.call-done = f32[60,128,128]{2,1,0:T(8,128)} async-done(((f32[1920,128,128]{2,1,0:T(8,128)}), f32[60,128,128]{2,1,0:T(8,128)}) %reduce-scatter.2.cloned.1.call-update) | async-done | bytes 3932176 | tf_op jit(solution)/shard_map/reduce_scatter | solution.py:363
  4001.3 705.1 %custom-call.10 = f32[60,128,128]{2,1,0:T(8,128)} custom-call(f32[60,128,128]{2,1,0:T(8,128)} %fusion.113), custom_call_target="Cholesky" | custom-call | tf_op jit(solution)/shard_map/cholesky/custom-call.1 | solution.py:101
  4729.9 705.1 %custom-call.8 = f32[60,128,128]{2,1,0:T(8,128)} custom-call(f32[60,128,128]{2,1,0:T(8,128)} %fusion.116), custom_call_target="Cholesky" | custom-call | tf_op jit(solution)/shard_map/cholesky/custom-call.1 | solution.py:101
  5444.8 590.8 %custom-call.9 = f32[60,1,128,128]{2,3,1,0:T(8,128)} custom-call(f32[60,1,128,128]{3,2,1,0:T(8,128)} %get-tuple-element.191), custom_call_target="InvertDiagBlocksLowerTriangular" | custom-call | tf_op jit(solution)/shard_map/triangular_solve/custom-call.0 | solution.py:102
  6052.6 591.0 %custom-call.11 = f32[60,1,128,128]{2,3,1,0:T(8,128)} custom-call(f32[60,1,128,128]{3,2,1,0:T(8,128)} %get-tuple-element.190), custom_call_target="InvertDiagBlocksLowerTriangular" | custom-call | tf_op jit(solution)/shard_map/triangular_solve/custom-call.0 | solution.py:102
  (667 shorter events, 1538.4 us)
Async XLA Ops:
  7.2 464.2 %all-gather.2.cloned.1.call-start = ((), (), s32[]{:S(2)}) async-start(), calls=%async_computation.7 | async-start | bytes 64880640 | tf_op jit(solution)/shard_map/all_gather | solution.py:217
  251.6 184.5 %copy-start.131 = (s32[32]{0:T(128)S(1)}, s32[32]{0:T(128)}, u32[]{:S(2)}) copy-start(s32[32]{0:T(128)} %param.20) | copy-start | bytes 388
  251.6 185.1 %copy-start.101 = (s32[1920]{0:T(1024)S(1)}, s32[1920]{0:T(1024)}, u32[]{:S(2)}) copy-start(s32[1920]{0:T(1024)} %param.22) | copy-start | bytes 23044
  255.0 195.4 %all-to-all-start.1 = ((bf16[32,32,1536]{2,1,0:T(8,128)(2,1)}), bf16[32,32,1536]{2,1,0:T(8,128)(2,1)S(1)}, u32[]{:S(2)}, u32[]{:S(2)}) async-start(bf16[32,32,1536]{2,1,0:T(8,128)(2,1)} %copy.238), calls=%async_computation.1 | async-start | bytes 6291456 | tf_op jit(solution)/shard_map/all_to_all | solution.py:234
  259.5 2954.7 %all-reduce.56.cloned.1.call-start = ((), (), s32[]{:S(2)}) async-start(), calls=%async_computation.9 | async-start | bytes 155648
  435.4 81.2 %copy-start.64 = (f32[19456]{0:T(1024)}, f32[19456]{0:T(1024)S(1)}, u32[]{:S(2)}) copy-start(f32[19456]{0:T(1024)S(1)} %convert_element_type.132) | copy-start | bytes 233476
  449.7 66.9 %copy-start.75 = (f32[1536]{0:T(1024)}, f32[1536]{0:T(1024)S(1)}, u32[]{:S(2)}) copy-start(f32[1536]{0:T(1024)S(1)} %get-tuple-element.174) | copy-start | bytes 18436
  450.3 97.9 %copy-start.67 = (f32[2048]{0:T(1024)}, f32[2048]{0:T(1024)S(1)}, u32[]{:S(2)}) copy-start(f32[2048]{0:T(1024)S(1)} %get-tuple-element.212) | copy-start | bytes 24580
  450.4 97.9 %copy-start.69 = (f32[2048]{0:T(1024)}, f32[2048]{0:T(1024)S(1)}, u32[]{:S(2)}) copy-start(f32[2048]{0:T(1024)S(1)} %get-tuple-element.209) | copy-start | bytes 24580
  450.4 97.9 %copy-start.71 = (f32[2048]{0:T(1024)}, f32[2048]{0:T(1024)S(1)}, u32[]{:S(2)}) copy-start(f32[2048]{0:T(1024)S(1)} %get-tuple-element.210) | copy-start | bytes 24580
  450.4 97.9 %copy-start.73 = (f32[2048]{0:T(1024)}, f32[2048]{0:T(1024)S(1)}, u32[]{:S(2)}) copy-start(f32[2048]{0:T(1024)S(1)} %get-tuple-element.211) | copy-start | bytes 24580
  450.4 144.3 %copy-start.54 = (f32[2048]{0:T(1024)}, f32[2048]{0:T(1024)S(1)}, u32[]{:S(2)}) copy-start(f32[2048]{0:T(1024)S(1)} %get-tuple-element.215) | copy-start | bytes 24580
  450.4 144.3 %copy-start.60 = (f32[2048]{0:T(1024)}, f32[2048]{0:T(1024)S(1)}, u32[]{:S(2)}) copy-start(f32[2048]{0:T(1024)S(1)} %get-tuple-element.168) | copy-start | bytes 24580
  450.4 144.3 %copy-start.62 = (f32[2048]{0:T(1024)}, f32[2048]{0:T(1024)S(1)}, u32[]{:S(2)}) copy-start(f32[2048]{0:T(1024)S(1)} %get-tuple-element.214) | copy-start | bytes 24580
  450.4 66.2 copy-start.4
  451.4 65.2 copy-start.83
  1146.2 37.4 copy-start.119
  1146.2 60.6 copy-start.14
  1146.3 263.9 %copy-start.81 = (f32[1024]{0:T(1024)}, f32[1024]{0:T(1024)S(1)}, u32[]{:S(2)}) copy-start(f32[1024]{0:T(1024)S(1)} %fusion.195) | copy-start | bytes 12292
  1146.3 37.3 copy-start.40
  1146.3 37.3 copy-start.115
  1367.0 43.1 copy-start.120
  1367.0 43.1 copy-start.116
  1790.3 35.1 slice-start.11
  1872.9 34.0 copy-start.57
  1872.9 34.0 copy-start.106
  1872.9 34.1 copy-start.50
  1872.9 34.1 copy-start.51
  1873.0 34.1 copy-start.104
  1873.0 34.3 copy-start.48
  1873.0 34.3 copy-start.102
  1873.0 34.4 copy-start.44
  1873.0 34.4 copy-start.45
  1873.0 34.5 copy-start.95
  2050.5 64.3 copy-start.55
  2050.5 64.3 copy-start.61
  2050.5 64.3 copy-start.63
  2050.5 64.3 copy-start.80
  2434.0 1473.4 %reduce-scatter.2.cloned.1.call-start = ((), (), s32[]{:S(2)}) async-start(), calls=%async_computation.8 | async-start | bytes 129761280 | tf_op jit(solution)/shard_map/reduce_scatter | solution.py:363
  2511.9 85.0 %copy-start.123 = (pred[1920]{0:T(1024)(128)(4,1)S(1)}, pred[1920]{0:T(1024)(128)(4,1)}, u32[]{:S(2)}) copy-start(pred[1920]{0:T(1024)(128)(4,1)} %broadcast_compare_fusion) | copy-start | bytes 5764
  2781.9 136.0 %all-to-all-start.2 = ((bf16[32,2,24576]{2,1,0:T(2,128)(2,1)}), bf16[32,2,24576]{2,1,0:T(2,128)(2,1)}, u32[]{:S(2)}, u32[]{:S(2)}) async-start(bf16[32,2,24576]{2,1,0:T(2,128)(2,1)} %reshape.1041), calls=%async_computation.2 | async-start | bytes 6291456 | tf_op jit(solution)/shard_map/all_to_all | solution.py:307
  2918.0 145.0 %all-to-all-start.4 = ((bf16[32,2,24576]{2,1,0:T(2,128)(2,1)}), bf16[32,2,24576]{2,1,0:T(2,128)(2,1)S(1)}, u32[]{:S(2)}, u32[]{:S(2)}) async-start(bf16[32,2,24576]{2,1,0:T(2,128)(2,1)} %reshape.1043), calls=%async_computation.4 | async-start | bytes 6291456 | tf_op jit(solution)/shard_map/all_to_all | solution.py:310
  3064.7 143.7 %all-to-all-start.3 = ((bf16[32,32,1536]{2,1,0:T(8,128)(2,1)}), bf16[32,32,1536]{2,1,0:T(8,128)(2,1)S(1)}, u32[]{:S(2)}, u32[]{:S(2)}) async-start(bf16[32,32,1536]{2,1,0:T(8,128)(2,1)} %copy.255), calls=%async_computation.3 | async-start | bytes 6291456 | tf_op jit(solution)/shard_map/all_to_all | solution.py:319
  3096.3 117.9 %copy-start.118 = (f32[608]{0:T(1024)S(1)}, f32[608]{0:T(1024)}, u32[]{:S(2)}) copy-start(f32[608]{0:T(1024)} %param.30) | copy-start | bytes 7300
  3096.3 117.9 %copy-start.128 = (f32[608]{0:T(1024)S(1)}, f32[608]{0:T(1024)}, u32[]{:S(2)}) copy-start(f32[608]{0:T(1024)} %param.31) | copy-start | bytes 7300
  3096.3 117.9 %copy-start.129 = (f32[608]{0:T(1024)S(1)}, f32[608]{0:T(1024)}, u32[]{:S(2)}) copy-start(f32[608]{0:T(1024)} %param.32) | copy-start | bytes 7300
  3208.3 699.1 %copy-start.24 = (bf16[32,32,1536]{2,1,0:T(8,128)(2,1)}, bf16[32,32,1536]{2,1,0:T(8,128)(2,1)S(1)}, u32[]{:S(2)}) copy-start(bf16[32,32,1536]{2,1,0:T(8,128)(2,1)S(1)} %all-to-all-done.3) | copy-start | bytes 9437188
  3208.3 146.5 %all-to-all-start.5 = ((bf16[32,32,1536]{2,1,0:T(8,128)(2,1)}), bf16[32,32,1536]{2,1,0:T(8,128)(2,1)}, u32[]{:S(2)}, u32[]{:S(2)}) async-start(bf16[32,32,1536]{2,1,0:T(8,128)(2,1)} %copy.265), calls=%async_computation.5 | async-start | bytes 6291456 | tf_op jit(solution)/shard_map/all_to_all | solution.py:326
  (105 other events, 1258.5 us)
Sparse Core Ops, SparseCore 0:
  11.4 459.9 all-gather.1
  2434.1 127.0 all-reduce.55
  2677.9 1229.5 reduce-scatter.1
where the time goes:
time: 6720 us; the launch traced here: 6670 us
  other arithmetic  3050 us (45%)
  local copies, waits for them, and re-layouts  1720 us (26%)
  waiting for transfers between devices  979 us (15%)
  matrix products  547 us (8%)
  blocking collectives  321 us (5%)
    another operation x6, other arithmetic, orthonormal(): lower_factor = lax.linalg.cholesky(gram_matrix)  1420 us
    another operation x4, other arithmetic, orthonormal(): lax.linalg.triangular_solve(lower_factor, matrix, left_side=False, lower=...  1190 us
    reduce_scatter x1, waiting for transfers between devices, body(): lax.psum_scatter(slot_grads, ('dp', 'owner'), scatter_dimension=0, tiled=...  553 us
    slice x66, local copies, waits for them, and re-layouts, body(): lax.associative_scan(combine, (later_keep, states_back), reverse=True, ax...  453 us
    slice x60, local copies, waits for them, and re-layouts, body(): states = lax.associative_scan(combine, (decays, driven), axis=1)[1]  256 us
    unnamed x322, local copies, waits for them, and re-layouts  225 us
    unnamed x1, blocking collectives  174 us
    all_to_all x1, blocking collectives, body(): lax.all_to_all(inputs, ('dp', 'owner'), split_axis=1, concat_axis=0, tile...  148 us
  transfers between devices with their start and end apart: 8, of which 6 were waited for; matrix products, arithmetic and copies ran while one was open for 9% of the time, Pallas kernels for 0%

commit v1 on v0

v1 whole, which is shorter than its diff:
```python
import functools
import math

import jax
import jax.numpy as jnp
from jax import lax
from jax.experimental import pallas as pl
from jax.experimental.pallas import tpu as pltpu
from jax.sharding import Mesh
from jax.sharding import PartitionSpec as P

D = 1536
R = 2048
F = 4608
KW = 4
STEP = 5
NT = 1904
E = 128

EPS = 1e-06
BETA_ONE = 0.5
BETA_TWO = 0.6
BETA_STAT = 0.5
RATE = 0.02
SMALL_RATE = 0.6
DECAY = 0.01
ADAM_EPS = 1e-08
HIGH = lax.Precision.HIGHEST

DT, RT, FT = D // E, R // E, F // E
AT_X = 0
AT_Y = DT * RT
AT_OUT = 2 * DT * RT
AT_REC = 3 * DT * RT
AT_INP = AT_REC + RT
AT_GATE = AT_INP + RT
AT_UP = AT_GATE + DT * FT
AT_DOWN = AT_UP + DT * FT

AXES = ("yx", "core", "owner")
BLOCK = 256
WIDE = BLOCK // E
FFN_BLOCK = 256
FFN_WIDE = FFN_BLOCK // E
CHUNK = 32
ROWS = 256
HIGH_ROWS = 512

BF = jnp.bfloat16
F32 = jnp.float32

NN = (((1,), (0,)), ((), ()))
NT_DIMS = (((1,), (1,)), ((), ()))
TN_DIMS = (((0,), (0,)), ((), ()))


def mm(left, right, dims=NN):
    return lax.dot_general(left, right, dims, preferred_element_type=F32)


def gelu_pair(x):
    c = math.sqrt(2.0 / math.pi)
    sq = x * x
    t = jnp.tanh(x * (c + (c * 0.044715) * sq))
    half = 0.5 + 0.5 * t
    slope = half + (0.5 * x) * (1.0 - t * t) * (c + (3.0 * c * 0.044715) * sq)
    return x * half, slope


def gelu_only(x):
    c = math.sqrt(2.0 / math.pi)
    return x * (0.5 + 0.5 * jnp.tanh(x * (c + (c * 0.044715) * (x * x))))


def minus_expm1(y, exp_y):
    poly = 1.0 + y * (1.0 / 7.0)
    for n in (6.0, 5.0, 4.0, 3.0, 2.0):
        poly = 1.0 + (y * (1.0 / n)) * poly
    return jnp.where(y > -0.35, -y * poly, 1.0 - exp_y)


def whole(shape):
    return pl.BlockSpec(shape, lambda *_: (0,) * len(shape), pipeline_mode=pl.Buffered(1))


ANY = pl.BlockSpec(memory_space=pl.ANY)


def wait_bytes(ref, sem):
    pltpu.make_async_copy(ref, ref, sem).wait()


def load_tile(pos, packed, tile, dst, row, col, sem):
    pltpu.make_async_copy(
        packed.at[pos[tile]], dst.at[pl.ds(row * E, E), pl.ds(col * E, E)], sem
    ).start()


def store_tile(pos, packed, tile, src, row, col, sem):
    pltpu.make_async_copy(
        src.at[pl.ds(row * E, E), pl.ds(col * E, E)], packed.at[pos[tile]], sem
    ).start()


def move_pair(move, pos, packed, ref, sem, firsts, across, row, wide=WIDE):
    for m, first in enumerate(firsts):
        for c in range(wide):
            move(pos, packed, first + row * across + c, ref, row, m * wide + c, sem)


def move_down(move, pos, packed, ref, sem, first, col, wide=WIDE):
    for r in range(wide):
        move(pos, packed, first + r * DT + col, ref, r, col, sem)


def move_heads(move, pos, packed, ref, sem, step):
    for h in range(WIDE):
        for base, col in ((AT_REC, 0), (AT_INP, 1)):
            move(pos, packed, base + step * WIDE + h, ref.at[h], 0, col, sem)


def load_xy(pos, packed, wxy, wo, sem, step, begin, count):
    at = step * WIDE
    for i in range(count):
        move_pair(load_tile, pos, packed, wxy, sem, (AT_X + at, AT_Y + at), RT, begin + i)
        move_down(load_tile, pos, packed, wo, sem, AT_OUT + at * DT, begin + i)


def wait_xy(wxy, wo, wri, sem):
    wait_bytes(wxy, sem)
    wait_bytes(wo, sem)
    wait_bytes(wri, sem)


def conv_chunk(ref, r, taps, bias):
    now = ref[pl.ds(r, CHUNK), :]
    before = ref[pl.ds(pl.multiple_of(jnp.maximum(r - 8, 0), 8), 8), :]
    ext = jnp.concatenate([jnp.where(r == 0, 0.0, before), now], axis=0)
    total = bias + taps[0:1] * now
    for k in range(1, KW):
        total = total + taps[k : k + 1] * ext[8 - k : 8 - k + CHUNK]
    return total


def heads_of(pre, part):
    return jnp.concatenate(
        [pre[:, h * 2 * E + part * E : h * 2 * E + (part + 1) * E] for h in range(WIDE)], axis=1
    )


def scan_chunk(a, b, carry, reverse):
    groups = CHUNK // 8
    shape = (groups, 8, a.shape[-1])
    a, b = a.reshape(shape), b.reshape(shape)
    row = lax.broadcasted_iota(jnp.int32, shape, 1)
    for d in (1, 2, 4):
        turn = 8 - d if reverse else d
        ok = row < 8 - d if reverse else row >= d
        a_far = pltpu.roll(a, turn, 1)
        b_far = pltpu.roll(b, turn, 1)
        b = b + a * jnp.where(ok, b_far, 0.0)
        a = a * jnp.where(ok, a_far, 1.0)
    out = [None] * groups
    for g in range(groups)[:: -1 if reverse else 1]:
        out[g] = b[g] + a[g] * carry
        carry = out[g][0:1] if reverse else out[g][7:8]
    return jnp.concatenate(out, axis=0), carry


def norm_rows(x):
    return lax.rsqrt(jnp.mean(x * x, axis=-1, keepdims=True) + EPS)


def temporal_forward_kernel(
    pos, packed, tokens, gain, params,
    branch, keep_out, u_out, p_out, q_out, ga_out, g_out, sg_out, conv_low, mixed, resid,
    normed, wxy, wo, wri, gate_pre, pre, sems,
):
    step = pl.program_id(0)
    last = pl.num_programs(0) - 1
    slot = lax.rem(step, 2)
    other = 1 - slot
    after = jnp.minimum(step + 1, last)
    length = tokens.shape[0]

    @pl.when(step == 0)
    def _():
        move_heads(load_tile, pos, packed, wri.at[0], sems.at[0], 0)
        load_xy(pos, packed, wxy.at[0], wo.at[0], sems.at[0], 0, 0, DT)

        def one(i, _):
            rows = pl.ds(pl.multiple_of(i * E, E), E)
            x = tokens[rows, :].astype(F32)
            normed[rows, :] = (x * norm_rows(x) * gain[...]).astype(BF)
            resid[rows, :] = x
            return 0

        lax.fori_loop(0, length // E, one, 0)

    wait_xy(wxy.at[slot], wo.at[slot], wri.at[slot], sems.at[slot])
    move_heads(load_tile, pos, packed, wri.at[other], sems.at[other], after)

    for c in range(length // HIGH_ROWS):
        rows = slice(c * HIGH_ROWS, (c + 1) * HIGH_ROWS)
        both = mm(normed[rows, :], wxy[slot])
        branch[rows, :] = both[:, :BLOCK]
        gate_pre[rows, :] = both[:, BLOCK:]
        half = DT // 2
        load_xy(pos, packed, wxy.at[other], wo.at[other], sems.at[other], after, c * half, half)
    values = params[...]

    def convolve(i, _):
        r = pl.multiple_of(i * CHUNK, CHUNK)
        conv_low[pl.ds(r, CHUNK), :] = conv_chunk(branch, r, values[0:4], values[4:5]).astype(BF)
        return 0

    lax.fori_loop(0, length // CHUNK, convolve, 0, unroll=2)
    for h in range(WIDE):
        pre[:, h * 2 * E : (h + 1) * 2 * E] = mm(conv_low[:, h * E : (h + 1) * E], wri[slot, h])

    row_in = lax.broadcasted_iota(jnp.int32, (CHUNK, BLOCK), 0)

    def recur(i, carry):
        rows = pl.ds(pl.multiple_of(i * CHUNK, CHUNK), CHUNK)
        recall = jax.nn.sigmoid(heads_of(pre[rows, :], 0) + values[5:6])
        admit = jax.nn.sigmoid(heads_of(pre[rows, :], 1) + values[6:7])
        log_keep = recall * values[7:8]
        keep = jnp.exp(log_keep)
        keep_sq = keep * keep
        gap = jnp.sqrt(minus_expm1(2.0 * log_keep, keep_sq))
        conv = conv_low[rows, :].astype(F32)
        ga = gap * admit
        driven = ga * conv
        state, carry_out = scan_chunk(keep, driven, carry, False)
        prior = jnp.where(row_in == 0, carry, pltpu.roll(state, 1, 0))
        g, slope = gelu_pair(gate_pre[rows, :])
        mixed[rows, :] = (state * g).astype(BF)
        g_out[rows, :] = g
        sg_out[rows, :] = state * slope
        keep_out[rows, :] = keep
        ga_out[rows, :] = ga
        q_out[rows, :] = driven * (1.0 - admit)
        u = (prior * keep - (admit * conv) * (keep_sq / gap)) * recall
        u_out[rows, :] = u
        p_out[rows, :] = u * ((1.0 - recall) * values[7:8])
        return carry_out

    lax.fori_loop(0, length // CHUNK, recur, jnp.zeros((1, BLOCK), F32), unroll=2)

    for c in range(D // ROWS):
        cols = slice(c * ROWS, (c + 1) * ROWS)
        resid[:, cols] += mm(mixed[...], wo[slot, :, cols])

    @pl.when(step == last)
    def _():
        wait_xy(wxy.at[other], wo.at[other], wri.at[other], sems.at[other])


def temporal_forward(pos, packed, tokens, gain, params):
    length = tokens.shape[0]
    column = pl.BlockSpec((length, BLOCK), lambda i, *_: (0, i))
    wide = jax.ShapeDtypeStruct((length, R), F32)
    low = jax.ShapeDtypeStruct((length, R), BF)
    *saved, resid = pl.pallas_call(
        temporal_forward_kernel,
        grid_spec=pltpu.PrefetchScalarGridSpec(
            num_scalar_prefetch=1,
            grid=(R // BLOCK,),
            in_specs=[
                ANY,
                whole((length, D)),
                whole((1, D)),
                pl.BlockSpec((16, BLOCK), lambda i, *_: (0, i)),
            ],
            out_specs=[column] * 10 + [whole((length, D))],
            scratch_shapes=[
                pltpu.VMEM((length, D), BF),
                pltpu.VMEM((2, D, 2 * BLOCK), BF),
                pltpu.VMEM((2, BLOCK, D), BF),
                pltpu.VMEM((2, WIDE, E, 2 * E), BF),
                pltpu.VMEM((length, BLOCK), F32),
                pltpu.VMEM((length, 2 * BLOCK), F32),
                pltpu.SemaphoreType.DMA((2,)),
            ],
        ),
        out_shape=[wide] * 8 + [low] * 2 + [jax.ShapeDtypeStruct((length, D), F32)],
        compiler_params=pltpu.CompilerParams(vmem_limit_bytes=56 << 20),
        cost_estimate=pl.CostEstimate(
            flops=2 * length * D * R * 3, bytes_accessed=110 << 20, transcendentals=6 * length * R
        ),
        name="temporal_forward",
    )(pos, packed, tokens, gain, params)
    return saved, resid


def load_ffn(pos, packed, wgu, wd, sem, step, begin, count):
    at = step * FFN_WIDE
    for i in range(count):
        move_pair(load_tile, pos, packed, wgu, sem, (AT_GATE + at, AT_UP + at), FT, begin + i, FFN_WIDE)
        move_down(load_tile, pos, packed, wd, sem, AT_DOWN + at * DT, begin + i, FFN_WIDE)


def ffn_kernel(
    pos, packed, resid, back, gain, grads, activation, resid_back, out_back, gain_grad,
    normed, normed_t, total, normed_back, wgu, wd, glu, gub, sgu, sd, low, load_sems, store_sems, sem,
):
    step = pl.program_id(0)
    last = pl.num_programs(0) - 1
    slot = lax.rem(step, 2)
    other = 1 - slot
    after = jnp.minimum(step + 1, last)
    length = resid.shape[0]

    @pl.when(step == 0)
    def _():
        load_ffn(pos, packed, wgu.at[0], wd.at[0], load_sems.at[0], 0, 0, DT)

        def one(i, _):
            rows = pl.ds(pl.multiple_of(i * E, E), E)
            x = resid[rows, :]
            n = x * norm_rows(x) * gain[...]
            normed[rows, :] = n.astype(BF)
            normed_t[:, rows] = n.T.astype(BF)
            total[rows, :] = x
            normed_back[rows, :] = jnp.zeros_like(x)
            return 0

        lax.fori_loop(0, length // E, one, 0)

    wait_bytes(wgu.at[slot], load_sems.at[slot])
    wait_bytes(wd.at[slot], load_sems.at[slot])

    for c in range(length // HIGH_ROWS):
        rows = slice(c * HIGH_ROWS, (c + 1) * HIGH_ROWS)
        acts = mm(normed[rows, :], wgu[slot])
        glu_back = mm(back[rows, :], wd[slot], NT_DIMS)
        up = acts[:, FFN_BLOCK:]
        g, slope = gelu_pair(acts[:, :FFN_BLOCK])
        glu[rows, :] = (g * up).astype(BF)
        gub[rows, :FFN_BLOCK] = (glu_back * up * slope).astype(BF)
        gub[rows, FFN_BLOCK:] = (glu_back * g).astype(BF)

    for c in range(D // ROWS):
        cols = slice(c * ROWS, (c + 1) * ROWS)
        total[:, cols] += mm(glu[...], wd[slot, :, cols])
        normed_back[:, cols] += mm(gub[...], wgu[slot, cols, :], NT_DIMS)
        load_ffn(pos, packed, wgu.at[other], wd.at[other], load_sems.at[other], after, c * 2, 2)

    @pl.when(step >= 2)
    def _():
        wait_bytes(sgu.at[slot], store_sems.at[slot])
        wait_bytes(sd.at[slot], store_sems.at[slot])

    at = step * FFN_WIDE
    out_sem = store_sems.at[slot]
    sd[slot] = mm(glu[...], back[...], TN_DIMS).astype(BF)
    for c in range(DT):
        move_down(store_tile, pos, grads, sd.at[slot], out_sem, AT_DOWN + at * DT, c, FFN_WIDE)
    half = D // 2
    for c in range(2):
        rows = slice(c * half, (c + 1) * half)
        sgu[slot, rows, :] = mm(normed_t[rows, :], gub[...]).astype(BF)
        for j in range(DT // 2):
            firsts = (AT_GATE + at, AT_UP + at)
            move_pair(store_tile, pos, grads, sgu.at[slot], out_sem, firsts, FT, c * (DT // 2) + j, FFN_WIDE)

    @pl.when(step == last)
    def _():
        def one(i, gain_sum):
            rows = pl.ds(pl.multiple_of(i * E, E), E)
            x = resid[rows, :]
            n_back = normed_back[rows, :]
            inv = norm_rows(x)
            scaled = n_back * gain[...]
            mean = jnp.mean(scaled * x, axis=-1, keepdims=True)
            x_back = back[rows, :].astype(F32) + (inv * scaled - x * (inv * inv * inv * mean))
            normed_back[rows, :] = x_back
            normed[rows, :] = x_back.astype(BF)
            low[rows, :] = total[rows, :].astype(BF)
            return gain_sum + jnp.sum((n_back * x * inv).reshape(E // 8, 8, D), axis=0)

        gain_sum = lax.fori_loop(0, length // E, one, jnp.zeros((8, D), F32))
        gain_grad[...] = jnp.sum(gain_sum, axis=0, keepdims=True)
        outs = [
            pltpu.make_async_copy(normed_back, resid_back, sem.at[0]),
            pltpu.make_async_copy(normed, out_back, sem.at[1]),
            pltpu.make_async_copy(low, activation, sem.at[2]),
        ]
        for copy in outs:
            copy.start()
        for copy in outs:
            copy.wait()
        wait_bytes(wgu.at[other], load_sems.at[other])
        wait_bytes(wd.at[other], load_sems.at[other])
        for s in range(2):
            wait_bytes(sgu.at[s], store_sems.at[s])
            wait_bytes(sd.at[s], store_sems.at[s])


def ffn(pos, packed, resid, back, gain):
    length = resid.shape[0]
    return pl.pallas_call(
        ffn_kernel,
        grid_spec=pltpu.PrefetchScalarGridSpec(
            num_scalar_prefetch=1,
            grid=(F // FFN_BLOCK,),
            in_specs=[ANY, whole((length, D)), whole((length, D)), whole((1, D))],
            out_specs=[ANY, ANY, ANY, ANY, whole((1, D))],
            scratch_shapes=[
                pltpu.VMEM((length, D), BF),
                pltpu.VMEM((D, length), BF),
                pltpu.VMEM((length, D), F32),
                pltpu.VMEM((length, D), F32),
                pltpu.VMEM((2, D, 2 * FFN_BLOCK), BF),
                pltpu.VMEM((2, FFN_BLOCK, D), BF),
                pltpu.VMEM((length, FFN_BLOCK), BF),
                pltpu.VMEM((length, 2 * FFN_BLOCK), BF),
                pltpu.VMEM((2, D, 2 * FFN_BLOCK), BF),
                pltpu.VMEM((2, FFN_BLOCK, D), BF),
                pltpu.VMEM((length, D), BF),
                pltpu.SemaphoreType.DMA((2,)),
                pltpu.SemaphoreType.DMA((2,)),
                pltpu.SemaphoreType.DMA((3,)),
            ],
        ),
        out_shape=[
            jax.ShapeDtypeStruct(packed.shape, BF),
            jax.ShapeDtypeStruct((length, D), BF),
            jax.ShapeDtypeStruct((length, D), F32),
            jax.ShapeDtypeStruct((length, D), BF),
            jax.ShapeDtypeStruct((1, D), F32),
        ],
        compiler_params=pltpu.CompilerParams(vmem_limit_bytes=60 << 20),
        cost_estimate=pl.CostEstimate(
            flops=18 * length * D * F, bytes_accessed=110 << 20, transcendentals=length * F
        ),
        name="ffn_both_ways",
    )(pos, packed, resid, back, gain)


def temporal_backward_kernel(
    pos, packed, grads_in, resid_back, tokens, out_back, gain, params,
    branch, keep_in, u_in, p_in, q_in, ga_in, g_in, sg_in, conv_low, mixed,
    grads, input_grad, gain_grad, small_grad,
    normed_t, normed_back, wxy, wo, wri, bp, ri, mixed_back, conv_back, resid_rows,
    sxy, so, sri, zeros, load_sems, store_sems, zero_sem, resid_sems,
):
    step = pl.program_id(0)
    last = pl.num_programs(0) - 1
    slot = lax.rem(step, 2)
    other = 1 - slot
    after = jnp.minimum(step + 1, last)
    length = tokens.shape[0]
    chunks = length // CHUNK
    empty = pos.shape[0] - NT

    @pl.when(step == 0)
    def _():
        move_heads(load_tile, pos, packed, wri.at[0], load_sems.at[0], 0)
        load_xy(pos, packed, wxy.at[0], wo.at[0], load_sems.at[0], 0, 0, DT)
        zeros[...] = jnp.zeros_like(zeros)
        for t in range(empty):
            pltpu.make_async_copy(zeros.at[t], grads.at[pos[NT + t]], zero_sem).start()

        def one(i, _):
            rows = pl.ds(pl.multiple_of(i * E, E), E)
            x = tokens[rows, :].astype(F32)
            normed_t[:, rows] = (x * norm_rows(x) * gain[...]).T.astype(BF)
            normed_back[rows, :] = jnp.zeros_like(x)
            return 0

        lax.fori_loop(0, length // E, one, 0)
        wait_bytes(zeros, zero_sem)

    wait_xy(wxy.at[slot], wo.at[slot], wri.at[slot], load_sems.at[slot])
    move_heads(load_tile, pos, packed, wri.at[other], load_sems.at[other], after)
    values = params[...]

    for c in range(length // HIGH_ROWS):
        rows = slice(c * HIGH_ROWS, (c + 1) * HIGH_ROWS)
        mixed_back[rows, :] = mm(out_back[rows, :], wo[slot], NT_DIMS)
        half = DT // 2
        load_xy(pos, packed, wxy.at[other], wo.at[other], load_sems.at[other], after, c * half, half)
    row_in = lax.broadcasted_iota(jnp.int32, (CHUNK, BLOCK), 0)

    def fold(v):
        return jnp.sum(v.reshape(CHUNK // 8, 8, BLOCK), axis=0)

    def recur(i, kept):
        keep_after, carry, rec_sum, inp_sum, decay_sum = kept
        rows = pl.ds(pl.multiple_of((chunks - 1 - i) * CHUNK, CHUNK), CHUNK)
        keep = keep_in[rows, :]
        later = jnp.where(row_in == CHUNK - 1, keep_after, pltpu.roll(keep, CHUNK - 1, 0))
        m_back = mixed_back[rows, :]
        bp[rows, BLOCK:] = (m_back * sg_in[rows, :]).astype(BF)
        carried, carry = scan_chunk(later, m_back * g_in[rows, :], carry, True)
        rec_back = carried * p_in[rows, :]
        inp_back = carried * q_in[rows, :]
        conv_back[rows, :] = carried * ga_in[rows, :]
        for h in range(WIDE):
            at = h * 2 * E
            ri[rows, at : at + E] = rec_back[:, h * E : (h + 1) * E].astype(BF)
            ri[rows, at + E : at + 2 * E] = inp_back[:, h * E : (h + 1) * E].astype(BF)
        return (
            keep[0:1],
            carry,
            rec_sum + fold(rec_back),
            inp_sum + fold(inp_back),
            decay_sum + fold(carried * u_in[rows, :]),
        )

    one_row = jnp.zeros((1, BLOCK), F32)
    eight = jnp.zeros((8, BLOCK), F32)
    _, _, rec_sum, inp_sum, decay_sum = lax.fori_loop(
        0, chunks, recur, (one_row, one_row, eight, eight, eight), unroll=2
    )
    small_grad[5:6, :] = jnp.sum(rec_sum, axis=0, keepdims=True)
    small_grad[6:7, :] = jnp.sum(inp_sum, axis=0, keepdims=True)
    small_grad[7:8, :] = jnp.sum(decay_sum, axis=0, keepdims=True) * values[8:9]

    @pl.when(step >= 2)
    def _():
        wait_xy(sxy.at[slot], so.at[slot], sri.at[slot], store_sems.at[slot])

    for h in range(WIDE):
        part = slice(h * 2 * E, (h + 1) * 2 * E)
        one_head = slice(h * E, (h + 1) * E)
        conv_back[:, one_head] += mm(ri[:, part], wri[slot, h], NT_DIMS)
        sri[slot, h] = mm(conv_low[:, one_head], ri[:, part], TN_DIMS).astype(BF)

    def unconvolve(i, sums):
        r = pl.multiple_of(i * CHUNK, CHUNK)
        rows = pl.ds(r, CHUNK)
        back = conv_back[rows, :]
        after_rows = conv_back[pl.ds(pl.multiple_of(jnp.minimum(r + CHUNK, length - 8), 8), 8), :]
        ext = jnp.concatenate([back, jnp.where(i == chunks - 1, 0.0, after_rows)], axis=0)
        now = branch[rows, :]
        total = values[0:1] * back
        out = [sums[0] + fold(back * now)]
        for k in range(1, KW):
            total = total + values[k : k + 1] * ext[k : k + CHUNK]
        bp[rows, :BLOCK] = total.astype(BF)
        before = branch[pl.ds(pl.multiple_of(jnp.maximum(r - 8, 0), 8), 8), :]
        prev = jnp.concatenate([jnp.where(r == 0, 0.0, before), now], axis=0)
        for k in range(1, KW):
            out.append(sums[k] + fold(back * prev[8 - k : 8 - k + CHUNK]))
        out.append(sums[KW] + fold(back))
        return tuple(out)

    sums = lax.fori_loop(0, chunks, unconvolve, (eight,) * (KW + 1), unroll=2)
    for k in range(KW + 1):
        small_grad[k : k + 1, :] = jnp.sum(sums[k], axis=0, keepdims=True)

    for c in range(D // ROWS):
        cols = slice(c * ROWS, (c + 1) * ROWS)
        normed_back[:, cols] += mm(bp[...], wxy[slot, cols, :], NT_DIMS)

    at = step * WIDE
    out_sem = store_sems.at[slot]
    so[slot] = mm(mixed[...], out_back[...], TN_DIMS).astype(BF)
    for c in range(DT):
        move_down(store_tile, pos, grads, so.at[slot], out_sem, AT_OUT + at * DT, c)
    half = D // 2
    for c in range(2):
        rows = slice(c * half, (c + 1) * half)
        sxy[slot, rows, :] = mm(normed_t[rows, :], bp[...]).astype(BF)
        for j in range(DT // 2):
            firsts = (AT_X + at, AT_Y + at)
            move_pair(store_tile, pos, grads, sxy.at[slot], out_sem, firsts, RT, c * (DT // 2) + j)
    move_heads(store_tile, pos, grads, sri.at[slot], out_sem, step)

    @pl.when(step == last)
    def _():
        def fetch(i):
            return pltpu.make_async_copy(
                resid_back.at[pl.ds(i * E, E)], resid_rows.at[i % 2], resid_sems.at[i % 2]
            )

        fetch(0).start()
        gain_sum = jnp.zeros((8, D), F32)
        for i in range(length // E):
            if i + 1 < length // E:
                fetch(i + 1).start()
            fetch(i).wait()
            rows = slice(i * E, (i + 1) * E)
            x = tokens[rows, :].astype(F32)
            n_back = normed_back[rows, :]
            inv = norm_rows(x)
            scaled = n_back * gain[...]
            mean = jnp.mean(scaled * x, axis=-1, keepdims=True)
            x_back = resid_rows[i % 2] + (inv * scaled - x * (inv * inv * inv * mean))
            input_grad[rows, :] = x_back.astype(BF)
            gain_sum = gain_sum + jnp.sum((n_back * x * inv).reshape(E // 8, 8, D), axis=0)
        gain_grad[...] = jnp.sum(gain_sum, axis=0, keepdims=True)
        wait_xy(wxy.at[other], wo.at[other], wri.at[other], load_sems.at[other])
        for s in range(2):
            wait_xy(sxy.at[s], so.at[s], sri.at[s], store_sems.at[s])


def temporal_backward(pos, packed, grads, resid_back, tokens, out_back, gain, params, saved):
    length = tokens.shape[0]
    column = pl.BlockSpec((length, BLOCK), lambda i, *_: (0, i))
    return pl.pallas_call(
        temporal_backward_kernel,
        grid_spec=pltpu.PrefetchScalarGridSpec(
            num_scalar_prefetch=1,
            grid=(R // BLOCK,),
            in_specs=[
                ANY, ANY, ANY,
                whole((length, D)), whole((length, D)), whole((1, D)),
                pl.BlockSpec((16, BLOCK), lambda i, *_: (0, i)),
            ]
            + [column] * 10,
            out_specs=[
                ANY,
                whole((length, D)),
                whole((1, D)),
                pl.BlockSpec((8, BLOCK), lambda i, *_: (0, i)),
            ],
            scratch_shapes=[
                pltpu.VMEM((D, length), BF),
                pltpu.VMEM((length, D), F32),
                pltpu.VMEM((2, D, 2 * BLOCK), BF),
                pltpu.VMEM((2, BLOCK, D), BF),
                pltpu.VMEM((2, WIDE, E, 2 * E), BF),
                pltpu.VMEM((length, 2 * BLOCK), BF),
                pltpu.VMEM((length, 2 * BLOCK), BF),
                pltpu.VMEM((length, BLOCK), F32),
                pltpu.VMEM((length, BLOCK), F32),
                pltpu.VMEM((2, E, D), F32),
                pltpu.VMEM((2, D, 2 * BLOCK), BF),
                pltpu.VMEM((2, BLOCK, D), BF),
                pltpu.VMEM((2, WIDE, E, 2 * E), BF),
                pltpu.VMEM((pos.shape[0] - NT, E, E), BF),
                pltpu.SemaphoreType.DMA((2,)),
                pltpu.SemaphoreType.DMA((2,)),
                pltpu.SemaphoreType.DMA,
                pltpu.SemaphoreType.DMA((2,)),
            ],
        ),
        out_shape=[
            jax.ShapeDtypeStruct(grads.shape, BF),
            jax.ShapeDtypeStruct((length, D), BF),
            jax.ShapeDtypeStruct((1, D), F32),
            jax.ShapeDtypeStruct((8, R), F32),
        ],
        input_output_aliases={2: 0},
        compiler_params=pltpu.CompilerParams(vmem_limit_bytes=60 << 20),
        cost_estimate=pl.CostEstimate(
            flops=12 * length * D * R, bytes_accessed=130 << 20, transcendentals=length * R
        ),
        name="temporal_backward",
    )(pos, packed, grads, resid_back, tokens, out_back, gain, params, *saved)


def lanes_last(src, dst):
    count, lanes = src.shape[0], dst.shape[2]

    def one(q, _):
        at = pl.multiple_of(q * 8, 8)
        part = jnp.swapaxes(src[:, pl.ds(at, 8), :], 0, 1)
        if count < lanes:
            part = jnp.concatenate([part, jnp.zeros((8, lanes - count, E), F32)], axis=1)
        for k in range(8):
            dst[at + k] = part[k].T
        return 0

    lax.fori_loop(0, src.shape[1] // 8, one, 0)


def lanes_first(src, dst):
    count = dst.shape[0]

    def one(q, _):
        at = pl.multiple_of(q * 8, 8)
        part = jnp.swapaxes(src[:, pl.ds(at, 8), :], 0, 1)
        turned = jnp.stack([part[i].T[:count] for i in range(8)], axis=0)
        dst[:, pl.ds(at, 8), :] = jnp.swapaxes(turned, 0, 1)
        return 0

    lax.fori_loop(0, src.shape[1] // 8, one, 0)


def solve_kernel(gram, rows, left, right, factor, solved, inverse):
    size, tall = gram.shape[1], 32
    lanes_last(gram, factor)

    def eliminate(ref, acc, r0, count, j0, begin):
        window = pl.ds(r0, count)

        def one(k, acc):
            col = ref[k, window, :]
            return tuple(
                acc[c] - col * factor[k, j0 + c : j0 + c + 1, :] for c in range(8)
            )

        def eight(q, acc):
            for u in range(8):
                acc = one(q * 8 + u, acc)
            return acc

        return lax.fori_loop(begin // 8, j0 // 8, eight, acc)

    def finish(ref, acc, r0, count, j0, scales):
        acc = list(acc)
        for c in range(8):
            for c2 in range(c):
                acc[c] = acc[c] - acc[c2] * factor[j0 + c2, j0 + c : j0 + c + 1, :]
            acc[c] = acc[c] * scales[c]
            ref[j0 + c, pl.ds(r0, count), :] = acc[c]

    for j0 in range(0, size, 8):
        acc = tuple(factor[j0 + c, j0 : j0 + 8, :] for c in range(8))
        cols = list(eliminate(factor, acc, j0, 8, j0, 0))
        scales = []
        for c in range(8):
            pivot = cols[c][c : c + 1]
            scale = lax.rsqrt(pivot)
            scale = scale * (1.5 - 0.5 * (pivot * scale) * scale)
            scales.append(scale)
            cols[c] = cols[c] * scale
            for c2 in range(c + 1, 8):
                cols[c2] = cols[c2] - cols[c] * cols[c][c2 : c2 + 1]
        for c in range(8):
            factor[j0 + c, j0 : j0 + 8, :] = cols[c]
        at = j0 + 8
        while at < size:
            count = min(tall, size - at)
            acc = tuple(factor[j0 + c, at : at + count, :] for c in range(8))
            acc = eliminate(factor, acc, at, count, j0, 0)
            finish(factor, acc, at, count, j0, scales)
            at += count
        for at in range(0, size, tall):
            if at > j0:
                for c in range(8):
                    solved[j0 + c, at : at + tall, :] = jnp.zeros((tall, solved.shape[2]), F32)
                continue
            row = lax.broadcasted_iota(jnp.int32, (tall, solved.shape[2]), 0) + at
            acc = tuple(jnp.where(row == j0 + c, 1.0, 0.0) for c in range(8))
            acc = eliminate(solved, acc, at, tall, j0, at)
            finish(solved, acc, at, tall, j0, scales)

    lanes_first(solved, inverse)
    slots = left.shape[0]

    def one(m, _):
        for side, out in enumerate((left, right)):
            at = side * slots + m
            out[m] = product(split3(rows[at]), split3(inverse[at]), NN, 3)
        return 0

    lax.fori_loop(0, slots, one, 0, unroll=2 if slots % 2 == 0 else 1)


def solve(gram, rows):
    count = gram.shape[0]
    spare = -count % 8
    if spare:
        gram = jnp.pad(gram, ((0, spare), (0, 0), (0, 0)))
    lanes = E * -(-count // E)
    vmem = pl.BlockSpec(memory_space=pltpu.VMEM)
    shape = jax.ShapeDtypeStruct((count // 2, E, E), F32)
    return pl.pallas_call(
        solve_kernel,
        out_shape=[shape, shape],
        in_specs=[vmem, vmem],
        out_specs=[vmem, vmem],
        scratch_shapes=[
            pltpu.VMEM((E, E, lanes), F32),
            pltpu.VMEM((E, E, lanes), F32),
            pltpu.VMEM(gram.shape, F32),
        ],
        compiler_params=pltpu.CompilerParams(vmem_limit_bytes=56 << 20),
        cost_estimate=pl.CostEstimate(
            flops=60 * 10**9, bytes_accessed=12 * gram.size, transcendentals=0
        ),
        name="cholesky_solve",
    )(gram, rows)


def split3(x):
    one = x.astype(BF)
    rest = x - one.astype(F32)
    two = rest.astype(BF)
    return one, two, (rest - two.astype(F32)).astype(BF)


def product(left, right, dims, terms):
    pairs = [(a, t - a) for t in range(terms - 1, -1, -1) for a in range(t + 1)]
    pairs = [(a, b) for a, b in pairs if a < len(left) and b < len(right)]
    (left_axis,), (right_axis,) = dims[0]
    return mm(
        jnp.concatenate([left[a] for a, _ in pairs], axis=left_axis),
        jnp.concatenate([right[b] for _, b in pairs], axis=right_axis),
        dims,
    )


def rotate_kernel(
    own, weights, first, second, left, right, left_stat, right_stat, *refs
):
    weight_new, first_new, second_new, left_stat_new, right_stat_new, gram, rows = refs[-7:]
    each = range(own.shape[0])
    grads = [split3(own[i])[:2] for i in each]
    lefts = [split3(left[i]) for i in each]
    rights = [split3(right[i]) for i in each]
    sides = (
        (left_stat, left_stat_new, lefts, NT_DIMS),
        (right_stat, right_stat_new, rights, TN_DIMS),
    )
    halves = [split3(product(lefts[i][:2], grads[i], TN_DIMS, 2))[:2] for i in each]
    squares = [[product(grads[i], grads[i], side[3], 2) for i in each] for side in sides]
    turned = [product(halves[i], rights[i][:2], NN, 2) for i in each]
    moved = [[None for i in each] for side in sides]
    for s, (stat, stat_new, basis, _) in enumerate(sides):
        for i in each:
            now = BETA_STAT * stat[i] + (1.0 - BETA_STAT) * squares[s][i]
            stat_new[i] = now
            moved[s][i] = product(split3(now), basis[i], NN, 3)
            rows[s, i] = moved[s][i]
    scaled = []
    for i in each:
        first_now = BETA_ONE * first[i] + (1.0 - BETA_ONE) * turned[i]
        second_now = BETA_TWO * second[i] + (1.0 - BETA_TWO) * turned[i] * turned[i]
        first_new[i] = first_now
        second_new[i] = second_now
        scaled.append(
            first_now
            / (1.0 - BETA_ONE**STEP)
            / (jnp.sqrt(second_now / (1.0 - BETA_TWO**STEP)) + ADAM_EPS)
        )
    back = [split3(product(lefts[i][:2], split3(scaled[i])[:2], NN, 2))[:2] for i in each]
    for s in range(2):
        for i in each:
            pieces = split3(moved[s][i])
            gram[s, i] = product(pieces, pieces, TN_DIMS, 3)
    for i in each:
        update = product(back[i], rights[i][:2], NT_DIMS, 2)
        weight_new[i] = weights[i] - RATE * (update + DECAY * weights[i])


def rotate(own, spans, states, before):
    slots = states[0].shape[0]
    count = sum(n for _, n in spans)
    group = max(g for g in (1, 2, 4) if all(b % g == 0 and n % g == 0 for b, n in spans))
    begin, size = spans[0][0] // group, spans[0][1] // group
    other = spans[-1][0] // group - size if len(spans) > 1 else begin

    def place(i):
        return (jnp.where(i < size, i + begin, i + other), 0, 0)

    block = pl.BlockSpec((group, E, E), place)
    pair = pl.BlockSpec((2, group, E, E), lambda i: (0, *place(i)))
    one = jax.ShapeDtypeStruct((slots, E, E), F32)
    two = jax.ShapeDtypeStruct((2, slots, E, E), F32)
    return pl.pallas_call(
        rotate_kernel,
        grid=(count // group,),
        in_specs=[pl.BlockSpec((group, E, E), lambda i: (i, 0, 0))] + [block] * 7 + [ANY] * len(before),
        out_specs=[block] * 5 + [pair] * 2,
        out_shape=[one] * 5 + [two] * 2,
        input_output_aliases={8 + i: i for i in range(len(before))},
        compiler_params=pltpu.CompilerParams(vmem_limit_bytes=50 << 20),
        cost_estimate=pl.CostEstimate(
            flops=count * 10**9, bytes_accessed=16 * 4 * count * E * E, transcendentals=0
        ),
        name="rotate",
    )(own, *states, *before)


def small_step(grads, weights, first_vals, second_vals):
    first_new = BETA_ONE * first_vals + (1.0 - BETA_ONE) * grads
    second_new = BETA_TWO * second_vals + (1.0 - BETA_TWO) * grads * grads
    scaled = (
        first_new
        / (1.0 - BETA_ONE**STEP)
        / (jnp.sqrt(second_new / (1.0 - BETA_TWO**STEP)) + ADAM_EPS)
    )
    return (weights - SMALL_RATE * scaled, first_new, second_new)


def small_tile(small):
    lead = small.shape[:-1]
    pad = [(0, 0)] * len(lead) + [(0, E * E - small.shape[-1])]
    return jnp.pad(small, pad).reshape(*lead, E, E)


def swap_pairs(size, bit):
    return [(i, i ^ bit) for i in range(size)]


def split_bits(chips):
    bits = [1 << b for b in range(chips.bit_length() - 1)]
    return bits[: len(bits) // 2], bits[len(bits) // 2 :]


def part_sizes(per_device):
    first = max(1, round(per_device / 15)) * 4
    second = 2 * first
    return [first, second], per_device - first - second


def block_of(along, across, size, other, half):
    edge = jnp.where(
        (across == 0) & (along > 0), 2 * along if half == 0 else 2 * (other - 1 + along), 0
    )
    edge = jnp.where(
        (across > 0) & (along == 0),
        2 * (size - 1 + across) if half == 0 else 2 * across,
        edge,
    )
    inner = 2 * (size + other - 1) + half * (size - 1) * (other - 1)
    inner = inner + (across - 1) * (size - 1) + along - 1
    return jnp.where((across > 0) & (along > 0), inner, edge + half)


def place_of_tile(holder, inner, per_device, chips, cores, owners):
    z, core, chip = holder % owners, holder // owners % cores, holder // (owners * cores)
    low, high = split_bits(chips)
    width, height = 1 << len(low), 1 << len(high)
    far = chip ^ lax.axis_index("yx")
    x, y = far % width, far // width
    far_core = core ^ lax.axis_index("core")
    far_z = (z - lax.axis_index("owner")) % owners
    sizes, rest = part_sizes(per_device)
    total, at = jnp.zeros_like(inner), 0
    for size in sizes:
        side = size // 2
        for half in range(2):
            args = (x, y, width, height, 0) if half == 0 else (y, x, height, width, 1)
            block = far_core * (2 * chips) + block_of(*args)
            place = at * chips * cores * owners + (block * owners + far_z) * side
            begin = at + half * side
            here = (inner >= begin) & (inner < begin + side)
            total = jnp.where(here, place + inner - begin, total)
        at += size
    place = at * chips * cores * owners + ((far_core * owners + far_z) * chips + far) * rest
    return jnp.where(inner >= at, place + inner - at, total)


def add_low(a, b):
    return (a.astype(F32) + b.astype(F32)).astype(BF)


def to_core(x):
    return lax.ppermute(x, "core", [(0, 1), (1, 0)])


def to_chip(x, chips, bit):
    return lax.ppermute(x, "yx", swap_pairs(chips, bit))


RIGHT = [(0, 1), (1, 2), (2, 3)]
LEFT = [(1, 0), (2, 1), (3, 2)]


def hop_one(x):
    return lax.ppermute(x, "owner", LEFT), lax.ppermute(x, "owner", RIGHT)


def hop_two(near, z):
    from_right = lax.ppermute(near[0], "owner", LEFT[:2])
    from_left = lax.ppermute(near[1], "owner", RIGHT[1:])
    return jnp.where(z < 2, from_right, from_left)


def hop_three(middle):
    return lax.ppermute(middle, "owner", [(1, 0), (2, 3)])


def line_join(x, near, middle, ends, z):
    return [x, jnp.where(z == 3, ends, near[0]), middle, jnp.where(z == 0, ends, near[1])]


def halves_first(blocks):
    side = blocks[0].shape[0] // 2
    return jnp.concatenate([b[:side] for b in blocks] + [b[side:] for b in blocks], axis=0)


def butterfly(x, bits, chips):
    pieces = [x]
    for bit in bits:
        pieces = pieces + [to_chip(p, chips, bit) for p in pieces]
    return pieces[1:]


def tie(*trees):
    return lax.optimization_barrier(trees)


def spread_chunk(joined, low, high, chips):
    half = joined.shape[0] // 2
    along_x = butterfly(joined, low, chips)
    along_y = butterfly(joined, high, chips)
    return along_x, along_y, half


def spread_rest(along_x, along_y, half, low, high, chips):
    inner = []
    for p in along_y:
        inner += butterfly(p[:half], low, chips)
    for p in along_x:
        inner += butterfly(p[half:], high, chips)
    return inner


def put(buffer, pieces, at):
    for piece in pieces:
        buffer = lax.dynamic_update_slice(buffer, piece, (at, 0, 0))
        at += piece.shape[0]
    return buffer


def gather_tiles(mine, chips, devices, beside):
    z = lax.axis_index("owner")
    low, high = split_bits(chips)
    per_device = mine.shape[0]
    (first, second), rest = part_sizes(per_device)
    one, two, three = mine[:first], mine[first : first + second], mine[first + second :]
    buffer = blank(devices * per_device)

    def join(x, near, middle, ends):
        return halves_first(line_join(x, near, middle, ends, z))

    near = hop_one(one)
    three = jnp.concatenate([three] + butterfly(three, low + high, chips), axis=0)
    middle = hop_two(near, z)
    middle, three = tie(middle, three)
    one = join(one, near, middle, hop_three(middle))
    one, two = tie(one, two)

    along_x, along_y, half = spread_chunk(one, low, high, chips)
    near = hop_one(two)
    middle = hop_two(near, z)
    along_x, along_y, middle = tie(along_x, along_y, middle)
    inner = spread_rest(along_x, along_y, half, low, high, chips)
    two = join(two, near, middle, hop_three(middle))
    pieces_one = [one] + along_x + along_y + inner
    two, pieces_one, three, beside = tie(two, pieces_one, three, beside)

    along_x, along_y, half = spread_chunk(two, low, high, chips)
    near = hop_one(three)
    middle = hop_two(near, z)
    joined = jnp.concatenate(pieces_one, axis=0)
    along_x, along_y, middle, joined = tie(along_x, along_y, middle, joined)
    inner = spread_rest(along_x, along_y, half, low, high, chips)
    ends = hop_three(middle)
    far_one = to_core(joined)
    edge = [two] + along_x + along_y
    buffer = put(buffer, [joined], 0)
    buffer = put(buffer, edge, first * devices)
    inner, ends, edge, beside, buffer = tie(inner, ends, edge, beside, buffer)

    beside = lax.all_to_all(beside, AXES, split_axis=0, concat_axis=0, tiled=True)
    pieces_three = line_join(three, near, middle, ends, z)
    far_two = [to_core(p) for p in edge + inner]
    far_even = to_core(jnp.concatenate(pieces_three[::2], axis=0))
    far_odd = to_core(jnp.concatenate(pieces_three[1::2], axis=0))
    size = three.shape[0]
    far_three = [far_even[:size], far_odd[:size], far_even[size:], far_odd[size:]]
    buffer = put(buffer, [far_one], joined.shape[0])
    at = first * devices + sum(p.shape[0] for p in edge)
    buffer = put(buffer, inner + far_two, at)
    return put(buffer, pieces_three + far_three, (first + second) * devices), beside


def fold_butterfly(blocks, bits, chips):
    for bit in bits[::-1]:
        far = [to_chip(b, chips, bit) for b in blocks[len(blocks) // 2 :]]
        blocks = [add_low(a, b) for a, b in zip(blocks, far)]
    return blocks[0]


def fold_one(x, z):
    x = x.reshape(4, -1, E, E)
    far = lax.ppermute(jnp.where(z == 0, x[3], x[1]), "owner", [(0, 1), (3, 2)])
    return x, add_low(x[2], far)


def fold_two(state):
    x, middle = state
    from_left = lax.ppermute(middle, "owner", RIGHT[:2])
    from_right = lax.ppermute(middle, "owner", LEFT[1:])
    return x[0], add_low(x[1], from_left), add_low(x[3], from_right)


def fold_three(state, last):
    mine, right, left = state
    from_left = lax.ppermute(right, "owner", RIGHT)
    from_right = lax.ppermute(left, "owner", LEFT)
    total = mine.astype(F32) + from_left.astype(F32) + from_right.astype(F32)
    return total if last else total.astype(BF)


def edge_blocks(chips, low, high):
    return 2 * ((1 << len(low)) + (1 << len(high)) - 1)


def fold_inner(edge, inner, low, high, chips):
    width, height = 1 << len(low), 1 << len(high)
    half = edge.shape[0] // edge_blocks(chips, low, high)
    edge, inner = edge.reshape(-1, half, E, E), inner.reshape(-1, half, E, E)
    along_x = [edge[2 * i : 2 * i + 2] for i in range(width)]
    along_y = [edge[2 * (width - 1 + i) : 2 * (width - 1 + i) + 2] for i in range(1, height)]
    for i in range(1, height):
        begin = (i - 1) * (width - 1)
        old = along_y[i - 1]
        blocks = [old[0]] + [inner[begin + j] for j in range(width - 1)]
        along_y[i - 1] = jnp.stack([fold_butterfly(blocks, low, chips), old[1]])
    for i in range(1, width):
        begin = (width - 1) * (height - 1) + (i - 1) * (height - 1)
        blocks = [along_x[i][1]] + [inner[begin + j] for j in range(height - 1)]
        along_x[i] = jnp.stack([along_x[i][0], fold_butterfly(blocks, high, chips)])
    return along_x[0], along_x[1:], along_y


def fold_outer(state, low, high, chips, owners):
    own, along_x, along_y = state
    zero = jnp.zeros_like(own)
    from_x = fold_butterfly([zero] + along_x, low, chips)
    from_y = fold_butterfly([zero] + along_y, high, chips)
    x = own.astype(F32) + from_x.astype(F32) + from_y.astype(F32)
    x = x.astype(BF).reshape(2, owners, -1, E, E)
    return x.transpose(1, 0, 2, 3, 4).reshape(-1, E, E)


def scatter_tiles(grads, chips, devices, owners):
    z = lax.axis_index("owner")
    low, high = split_bits(chips)
    per_device = grads.shape[0] // devices
    (first, second), rest = part_sizes(per_device)

    def cut(begin, size):
        halfway = size * devices // 2
        edge = halfway // (2 * chips) * edge_blocks(chips, low, high)
        at = begin * devices
        cuts = [at, at + edge, at + halfway, at + halfway + edge, at + 2 * halfway]
        return [grads[a:b] for a, b in zip(cuts, cuts[1:])]

    one, two = cut(0, first), cut(first, second)
    three = grads[(first + second) * devices :].reshape(2, -1, E, E)

    got_inner = to_core(two[3])
    got_inner, far = tie(got_inner, two[2])
    got_edge = to_core(far)
    got_edge, far_one, far_three = tie(got_edge, one[2:], three[1])
    got_three, got_one = to_core(far_three), [to_core(x) for x in far_one]
    two_inner = add_low(two[1], got_inner)
    two = fold_inner(add_low(two[0], got_edge), two_inner, low, high, chips)
    three = fold_one(add_low(three[0], got_three), z)
    two, got_one = tie(two, got_one)

    two = fold_outer(two, low, high, chips, owners)
    three = fold_two(three)
    three = fold_three(three, False)
    two, three = tie(two, three)

    one = [add_low(a, b) for a, b in zip(one, got_one)]
    one = fold_inner(one[0], one[1], low, high, chips)
    two = fold_one(two, z)
    two = fold_two(two)
    one = fold_outer(one, low, high, chips, owners)
    two = fold_three(two, True)
    one, two = tie(one, two)

    blocks = list(three.reshape(chips, -1, E, E))
    bits = low + high
    for bit in bits[::-1]:
        moved = [to_chip(b, chips, bit) for b in blocks[len(blocks) // 2 :]]
        blocks = [
            a.astype(F32) + b.astype(F32) if bit == bits[0] else add_low(a, b)
            for a, b in zip(blocks, moved)
        ]
    one = fold_three(fold_two(fold_one(one, z)), True)
    return two, jnp.concatenate([one, blocks[0]], axis=0)


def blank_kernel(out):
    pass


def blank(count):
    return pl.pallas_call(
        blank_kernel,
        out_shape=jax.ShapeDtypeStruct((count, E, E), BF),
        out_specs=ANY,
        name="blank",
    )()


def body(
    inputs,
    cotangent,
    lengths,
    balance,
    owner_slot_tile,
    master,
    first_moment,
    second_moment,
    left_basis,
    right_basis,
    left_stat,
    right_stat,
    small_master,
    small_first,
    small_second,
):
    yx, cores, owners = (lax.axis_size(name) for name in AXES)
    devices = yx * cores * owners
    rank = lax.axis_index(AXES)
    tokens = inputs[0]
    seq_len = tokens.shape[0]
    held = master.shape[0]
    small_held = small_master.shape[0]
    per_device = held + 1

    place_args = (per_device, yx, cores, owners)

    slots = jnp.arange(owner_slot_tile.shape[0], dtype=jnp.int32)
    place = place_of_tile(slots // held, slots % held, *place_args)
    hit = owner_slot_tile[:, None] == slots[None, :]
    pos = jnp.sum(jnp.where(hit, place[:, None], 0), axis=0)
    ranks = jnp.arange(devices, dtype=jnp.int32)
    small_place = place_of_tile(ranks, jnp.full_like(ranks, held), *place_args)

    mine = jnp.concatenate([master.astype(BF), small_tile(small_master.astype(BF))[None]], axis=0)
    shares = cotangent.reshape(devices, seq_len // devices, D)
    mine, pos = tie(mine, pos)
    packed, spread = gather_tiles(mine, yx, devices, shares)

    used = -(-small_held // E)
    small = packed[:, :used][small_place].reshape(devices, used * E)[:, :small_held]
    small = small.reshape(-1).astype(F32)
    gain_one, gain_two = small[None, :D], small[None, D : 2 * D]
    wide = small[2 * D :].reshape(KW + 4, R)
    decay_log = wide[KW + 3]
    params = jnp.concatenate(
        [
            wide[: KW + 3],
            -8.0 * jax.nn.softplus(-decay_log)[None],
            8.0 * jax.nn.sigmoid(-decay_log)[None],
            jnp.zeros((16 - KW - 5, R), F32),
        ],
        axis=0,
    )

    place_of = jnp.sum(
        jnp.where(
            balance[:, None] == jnp.arange(devices, dtype=jnp.int32)[None, :],
            jnp.arange(devices, dtype=jnp.int32)[:, None],
            0,
        ),
        axis=0,
    )
    params, spread = tie(params, spread)
    back = lax.all_to_all(spread[place_of], AXES, split_axis=0, concat_axis=0, tiled=True)
    live = jnp.arange(seq_len, dtype=jnp.int32) < lengths[rank]
    back = jnp.where(live[:, None], back.reshape(seq_len, D), 0).astype(BF)

    saved, resid = temporal_forward(pos, packed, tokens, gain_one, params)
    grads, activation, resid_back, out_back, grad_gain_two = ffn(pos, packed, resid, back, gain_two)
    grads, input_grad, grad_gain_one, small_grad = temporal_backward(
        pos, packed, grads, resid_back, tokens, out_back, gain_one, params, saved
    )

    small_grads = jnp.concatenate(
        [grad_gain_one.reshape(-1), grad_gain_two.reshape(-1), small_grad.reshape(-1)], axis=0
    )
    small_tiles = small_tile(small_grads.reshape(devices, small_held)).astype(BF)
    grads = grads.at[small_place].set(small_tiles)
    own_two, own_one = scatter_tiles(grads, yx, devices, owners)
    own_small = own_one[-1].reshape(-1)[:small_held]

    (first, second), _ = part_sizes(per_device)
    states = (
        master, first_moment, second_moment, left_basis, right_basis, left_stat, right_stat
    )
    spans_two = [(first, second)]
    spans_one = [(0, first), (first + second, held - first - second)]
    news = rotate(own_two, spans_two, states, ())
    *news, gram, rows = rotate(own_one, spans_one, states, news)
    new_left, new_right = solve(gram.reshape(-1, E, E), rows.reshape(-1, E, E))
    new_master, new_first, new_second, new_left_stat, new_right_stat = news

    small_new, small_first_new, small_second_new = small_step(
        own_small, small_master, small_first, small_second
    )
    return (
        activation[None],
        input_grad[None],
        new_master,
        new_first,
        new_second,
        new_left,
        new_right,
        new_left_stat,
        new_right_stat,
        small_new,
        small_first_new,
        small_second_new,
    )


def solution(mesh):
    dp, owner = mesh.devices.shape
    fine = Mesh(mesh.devices.reshape(dp // 2, 2, owner), AXES)
    cut = P(AXES)
    return jax.shard_map(
        body,
        mesh=fine,
        in_specs=(cut, cut, P(), P(), P()) + (cut,) * 10,
        out_specs=(cut,) * 12,
        check_vma=False,
    )
```

time: 6720 us -> 1150 us (0.17)
  other arithmetic: 3050 us -> 99 us
  local copies, waits for them, and re-layouts: 1720 us -> 154 us
  waiting for transfers between devices: 979 us -> 325 us
  matrix products: 547 us -> 0 us
  Pallas kernels: 0 us -> 433 us
  blocking collectives: 321 us -> 0 us
  starting transfers between devices: 37.4 us -> 121 us
    another operation x10 -> x7, other arithmetic: 2600 us -> 8.31 us  [the longest x3 4.69 us: fold_inner(): along_y[i - 1] = jnp.stack([fold_butterfly(blocks, low, chips), old[1]])]
    slice x130 -> x23, local copies, waits for them, and re-layouts: 755 us -> 46.4 us  [the longest x4 20.4 us: cut(): return [grads[a:b] for a, b in zip(cuts, cuts[1:])]]
    reduce_scatter x1 -> x0, waiting for transfers between devices: 553 us -> none  [body(): lax.psum_scatter(slot_grads, ('dp', 'owner'), scatter_dimension=0, tiled=...]
    dot_general x37 -> x0, matrix products: 524 us -> none  [the longest x6 146 us: back_product(): lax.dot_general(rows, weight, (((1,), (1,)), ((), ())), preferred_element...]
    pallas_call x0 -> x7, Pallas kernels: none -> 433 us  [the longest x1 167 us: ffn(): pl.pallas_call(ffn_kernel, grid_spec=pltpu.PrefetchScalarGridSpec(num_sca...]
    all_to_all x5 -> x2, waiting for transfers between devices: 409 us -> 7.52 us  [the longest x1 7.52 us: gather_tiles(): lax.all_to_all(beside, AXES, split_axis=0, concat_axis=0, tiled=True)]
    ppermute x0 -> x65, waiting for transfers between devices: none -> 318 us  [the longest x22 63.8 us: to_chip(): return lax.ppermute(x, 'yx', swap_pairs(chips, bit))]
    pad x36 -> x0, local copies, waits for them, and re-layouts: 208 us -> none  [the longest x18 104 us: body(): lax.associative_scan(combine, (later_keep, states_back), reverse=True, ax...]
  transfers between devices with their start and end apart: 8 -> 67, of which waited for: 6 -> 39; matrix products, arithmetic and copies ran while one was open for 9% -> 20% of each run, Pallas kernels for 0% -> 8%
where the time goes in v1:
time: 1150 us; the launch traced here: 1140 us
  Pallas kernels  433 us (38%)
  waiting for transfers between devices  325 us (28%)
  local copies, waits for them, and re-layouts  154 us (13%)
  starting transfers between devices  121 us (11%)
  other arithmetic  99 us (9%)
    pallas_call x1, Pallas kernels, ffn(): pl.pallas_call(ffn_kernel, grid_spec=pltpu.PrefetchScalarGridSpec(num_sca...  167 us
    pallas_call x1, Pallas kernels, temporal_backward(): pl.pallas_call(temporal_backward_kernel, grid_spec=pltpu.PrefetchScalarGr...  90.6 us
    pallas_call x1, Pallas kernels, temporal_forward(): pl.pallas_call(temporal_forward_kernel, grid_spec=pltpu.PrefetchScalarGri...  74.1 us
    dynamic_update_slice x18, local copies, waits for them, and re-layouts, put(): buffer = lax.dynamic_update_slice(buffer, piece, (at, 0, 0))  70.6 us
    pallas_call x1, Pallas kernels, solve(): pl.pallas_call(solve_kernel, out_shape=[shape, shape], in_specs=[vmem, vm...  66.3 us
    ppermute x22, waiting for transfers between devices, to_chip(): return lax.ppermute(x, 'yx', swap_pairs(chips, bit))  63.8 us
    ppermute x3, waiting for transfers between devices, fold_two(): from_right = lax.ppermute(middle, 'owner', LEFT[1:])  63 us
    convert_element_type x12, other arithmetic, add_low(): return (a.astype(F32) + b.astype(F32)).astype(BF)  49.4 us
  transfers between devices with their start and end apart: 67, of which 39 were waited for; matrix products, arithmetic and copies ran while one was open for 20% of the time, Pallas kernels for 8%

profile of v1, /device:TPU:16, one launch (start us, length us, event | category | flops | bytes accessed | tf_op | source)
XLA Modules:
  0.0 1135.4 jit_solution(16985435338031295532)
XLA Ops:
  15.7 8.0 collective-permute-done.4
  45.6 6.6 collective-permute-done.7
  63.9 15.5 %collective-permute-done.12 = bf16[32,128,128]{2,1,0:T(8,128)(2,1)S(1)} collective-permute-done((bf16[32,128,128]{2,1,0:T(8,128)(2,1)S(1)}, bf16[32,128,128]{2,1,0:T(8,128)(2,1)S(1)}, u32[]{:S(2)}, u32[]{:S(2)}) %collective-permute-start.12) | collective-permute-done | bytes 1048608 | tf_op jit(solution)/shard_map/ppermute | solution.py:958
  85.5 16.5 %collective-permute-done.13 = bf16[32,128,128]{2,1,0:T(8,128)(2,1)S(1)} collective-permute-done((bf16[32,128,128]{2,1,0:T(8,128)(2,1)S(1)}, bf16[32,128,128]{2,1,0:T(8,128)(2,1)S(1)}, u32[]{:S(2)}, u32[]{:S(2)}) %collective-permute-start.13) | collective-permute-done | bytes 1048608 | tf_op jit(solution)/shard_map/ppermute | solution.py:963
  113.3 12.4 %collective-permute-done.14 = bf16[32,128,128]{2,1,0:T(8,128)(2,1)S(1)} collective-permute-done((bf16[32,128,128]{2,1,0:T(8,128)(2,1)S(1)}, bf16[32,128,128]{2,1,0:T(8,128)(2,1)S(1)}, u32[]{:S(2)}, u32[]{:S(2)}) %collective-permute-start.14) | collective-permute-done | bytes 1048608 | tf_op jit(solution)/shard_map/ppermute | solution.py:968
  134.8 4.4 collective-permute-start.21
  141.1 30.9 %collective-permute-done.21 = bf16[52,128,128]{2,1,0:T(8,128)(2,1)S(1)} collective-permute-done((bf16[52,128,128]{2,1,0:T(8,128)(2,1)S(1)}, bf16[52,128,128]{2,1,0:T(8,128)(2,1)S(1)}, u32[]{:S(2)}, u32[]{:S(2)}) %collective-permute-start.21) | collective-permute-done | bytes 1703968 | tf_op jit(solution)/shard_map/ppermute | solution.py:958
  172.0 4.4 collective-permute-start.22
  185.0 19.8 %collective-permute-done.22 = bf16[52,128,128]{2,1,0:T(8,128)(2,1)S(1)} collective-permute-done((bf16[52,128,128]{2,1,0:T(8,128)(2,1)S(1)}, bf16[52,128,128]{2,1,0:T(8,128)(2,1)S(1)}, u32[]{:S(2)}, u32[]{:S(2)}) %collective-permute-start.22) | collective-permute-done | bytes 1703968 | tf_op jit(solution)/shard_map/ppermute | solution.py:963
  206.9 13.4 %collective-permute-done.18 = bf16[128,128,128]{2,1,0:T(8,128)(2,1)} collective-permute-done((bf16[128,128,128]{2,1,0:T(8,128)(2,1)}, bf16[128,128,128]{2,1,0:T(8,128)(2,1)}, u32[]{:S(2)}, u32[]{:S(2)}) %collective-permute-start.18) | collective-permute-done | bytes 4194336 | tf_op jit(solution)/shard_map/ppermute | solution.py:950
  232.9 10.4 constant_dynamic-update-slice_fusion.20
  243.4 4.8 constant_dynamic-update-slice_fusion.19
  248.1 4.8 constant_dynamic-update-slice_fusion.18
  253.0 4.8 constant_dynamic-update-slice_fusion.17
  257.7 10.5 collective-permute-done.25
  268.3 6.7 collective-permute-done.24
  279.2 5.4 all-to-all-start
  284.6 10.5 constant_dynamic-update-slice_fusion.16
  301.9 4.7 constant_dynamic-update-slice_fusion.13
  306.7 4.7 constant_dynamic-update-slice_fusion.12
  311.4 4.8 constant_dynamic-update-slice_fusion.11
  346.7 7.5 all-to-all-done
  358.5 5.9 all-to-all-start.1
  366.9 74.1 %temporal_forward.1 = (f32[1024,2048]{1,0:T(8,128)}, f32[1024,2048]{1,0:T(8,128)}, f32[1024,2048]{1,0:T(8,128)}, f32[1024,2048]{1,0:T(8,128)}, f32[1024,2048]{1,...) custom-call(s32[1920]{0:T(1024)} %select_reduce_fusion.pos, ...), custom_call_target="tpu_custom_call" | custom-call | flops 19327352832 | bytes 115343360 | tf_op jit(solution)/shard_map/temporal_forward/pallas_call | solution.py:264
  443.2 166.7 %ffn_both_ways.1 = (bf16[1952,128,128]{2,1,0:T(8,128)(2,1)}, bf16[1024,1536]{1,0:T(8,128)(2,1)}, f32[1024,1536]{1,0:T(8,128)}, bf16[1024,1536]{1,0:T(8,128)(2,1)}, f32[1,1536]{1,0:T(1,128)}) custom-call(s32[1920]{0:T(1024)} %select_reduce_fusion.pos, bf16[1952,128,128]{2,1,0:T(8,128)(2,1)} %slice_dynamic-update-slice_fusion.packed, ...), custom_call_target="tpu_custom_call" | custom-call | flops 130459631616 | bytes 115343360 | tf_op jit(solution)/shard_map/ffn_both_ways/pallas_call | solution.py:402
  610.0 90.6 %temporal_backward.1 = (bf16[1952,128,128]{2,1,0:T(8,128)(2,1)}, bf16[1024,1536]{1,0:T(8,128)(2,1)}, f32[1,1536]{1,0:T(1,128)}, f32[8,2048]{1,0:T(8,128)}) custom-call(s32[1920]{0:T(1024)} %select_reduce_fusion.pos, bf16[1952,128,128]{2,1,0:T(8,128)(2,1)} %slice_dynamic-update-slice_fusion.packed, ...), custom_call_target="tpu_custom_call", output_to_operand_aliasing={{0}: (2, {})} | custom-call | flops 38654705664 | bytes 136314880 | tf_op jit(solution)/shard_map/temporal_backward/pallas_call | solution.py:603
  702.6 4.6 scatter_fusion
  710.0 6.7 slice.393
  722.1 8.0 slice.394
  730.2 8.6 slice.396
  739.3 5.3 add_convert_fusion.4
  749.8 15.7 %add_convert_fusion = bf16[384,128,128]{2,1,0:T(8,128)(2,1)} fusion(bf16[384,128,128]{2,1,0:T(8,128)(2,1)} %collective-permute-done.35, bf16[1952,128,128]{2,1,0:T(8,128)(2,1)} %scatter_fusion), kind=kLoop, calls=%fused_computation.3 | loop fusion | flops 25165824 | bytes 37748736 | tf_op jit(solution)/shard_map/convert_element_type | solution.py:942
  765.6 12.5 %add_convert_fusion.1 = bf16[208,128,128]{2,1,0:T(8,128)(2,1)} fusion(bf16[208,128,128]{2,1,0:T(8,128)(2,1)} %collective-permute-done.46, bf16[1952,128,128]{2,1,0:T(8,128)(2,1)} %scatter_fusion), kind=kLoop, calls=%fused_computation.6 | loop fusion | flops 13631488 | bytes 20447232 | tf_op jit(solution)/shard_map/convert_element_type | solution.py:942
  786.0 8.9 collective-permute-done.37
  803.2 19.9 %collective-permute-done.47 = bf16[52,128,128]{2,1,0:T(8,128)(2,1)S(1)} collective-permute-done((bf16[52,128,128]{2,1,0:T(8,128)(2,1)}, bf16[52,128,128]{2,1,0:T(8,128)(2,1)S(1)}, u32[]{:S(2)}, u32[]{:S(2)}) %collective-permute-start.47) | collective-permute-done | bytes 1703968 | tf_op jit(solution)/shard_map/ppermute | solution.py:1076
  827.4 37.1 %collective-permute-done.50 = bf16[52,128,128]{2,1,0:T(8,128)(2,1)S(1)} collective-permute-done((bf16[52,128,128]{2,1,0:T(8,128)(2,1)S(1)}, bf16[52,128,128]{2,1,0:T(8,128)(2,1)S(1)}, u32[]{:S(2)}, u32[]{:S(2)}) %collective-permute-start.50) | collective-permute-done | bytes 1703968 | tf_op jit(solution)/shard_map/ppermute | solution.py:1083
  879.3 13.2 %collective-permute-done.44 = bf16[2,64,128,128]{3,2,1,0:T(8,128)(2,1)S(1)} collective-permute-done((bf16[2,64,128,128]{3,2,1,0:T(8,128)(2,1)S(1)}, bf16[2,64,128,128]{3,2,1,0:T(8,128)(2,1)S(1)}, u32[]{:S(2)}, u32[]{:S(2)}) %collective-permute-start.44) | collective-permute-done | bytes 4194336 | tf_op jit(solution)/shard_map/ppermute | solution.py:950
  895.3 8.3 add_convert_fusion.3
  916.9 7.5 add_convert_fusion.2
  928.6 11.9 %collective-permute-done.52 = bf16[32,128,128]{2,1,0:T(8,128)(2,1)} collective-permute-done((bf16[32,128,128]{2,1,0:T(8,128)(2,1)}, bf16[32,128,128]{2,1,0:T(8,128)(2,1)}, u32[]{:S(2)}, u32[]{:S(2)}) %collective-permute-start.52) | collective-permute-done | bytes 1048608 | tf_op jit(solution)/shard_map/ppermute | solution.py:1076
  946.9 19.2 %collective-permute-done.55 = bf16[32,128,128]{2,1,0:T(8,128)(2,1)S(1)} collective-permute-done((bf16[32,128,128]{2,1,0:T(8,128)(2,1)S(1)}, bf16[32,128,128]{2,1,0:T(8,128)(2,1)S(1)}, u32[]{:S(2)}, u32[]{:S(2)}) %collective-permute-start.55) | collective-permute-done | bytes 1048608 | tf_op jit(solution)/shard_map/ppermute | solution.py:1083
  980.2 7.2 collective-permute-done.63
  996.8 11.5 %collective-permute-done.57 = bf16[16,128,128]{2,1,0:T(8,128)(2,1)S(1)} collective-permute-done((bf16[16,128,128]{2,1,0:T(8,128)(2,1)S(1)}, bf16[16,128,128]{2,1,0:T(8,128)(2,1)S(1)}, u32[]{:S(2)}, u32[]{:S(2)}) %collective-permute-start.57) | collective-permute-done | bytes 524320 | tf_op jit(solution)/shard_map/ppermute | solution.py:1076
  1012.7 6.7 collective-permute-done.60
  1019.5 6.7 collective-permute-done.58
  1032.5 18.9 %rotate.2 = (f32[60,128,128]{2,1,0:T(8,128)}, f32[60,128,128]{2,1,0:T(8,128)}, f32[60,128,128]{2,1,0:T(8,128)}, f32[60,128,128]{2,1,0:T(8,128)}, f32[60,128,128]...) custom-call(f32[32,128,128]{2,1,0:T(8,128)S(1)} %convert_add_fusion.1.own, ...), custom_call_target="tpu_custom_call" | custom-call | flops 32000000000 | bytes 33554432 | tf_op jit(solution)/shard_map/rotate/pallas_call | solution.py:856
  1051.8 16.8 %rotate.3 = (f32[60,128,128]{2,1,0:T(8,128)}, f32[60,128,128]{2,1,0:T(8,128)}, f32[60,128,128]{2,1,0:T(8,128)}, f32[60,128,128]{2,1,0:T(8,128)}, f32[60,128,128]...) custom-call(f32[29,128,128]{2,1,0:T(8,128)S(1)} %pad_maximum_fusion., ...), custom_call_target="tpu_custom_call", output_to_operand_aliasing={{0}: (8, {}), {1}: (9, {}), {2}: (10, {}), {3}: (11, {}), {... | custom-call | flops 28000000000 | bytes 29360128 | tf_op jit(solution)/shard_map/rotate/pallas_call | solution.py:856
  1068.6 66.3 %cholesky_solve.1 = (f32[60,128,128]{2,1,0:T(8,128)}, f32[60,128,128]{2,1,0:T(8,128)}) custom-call(f32[120,128,128]{2,1,0:T(8,128)} %bitcast.83, f32[120,128,128]{2,1,0:T(8,128)} %bitcast.84), custom_call_target="tpu_custom_call" | custom-call | flops 60000002048 | bytes 23592960 | tf_op jit(solution)/shard_map/cholesky_solve/pallas_call | solution.py:763
  (288 shorter events, 262.4 us)
Async XLA Ops:
  54.9 24.6 %collective-permute-start.12 = (bf16[32,128,128]{2,1,0:T(8,128)(2,1)S(1)}, bf16[32,128,128]{2,1,0:T(8,128)(2,1)S(1)}, u32[]{:S(2)}, u32[]{:S(2)}) collective-permute-start(bf16[32,128,128]{2,1,0:T(8,128)(2,1)S(1)} %slice.301), channel_id=1, source_target_pairs={{0,1},{1,2},{2,3},{4,5},{5,6},{6,7},{8,9},{9,10},{10,11},{12,13},{... | collective-permute-start | bytes 3145736 | tf_op jit(solution)/shard_map/ppermute | solution.py:958
  59.2 23.3 %collective-permute-start.10 = (bf16[32,128,128]{2,1,0:T(8,128)(2,1)S(1)}, bf16[32,128,128]{2,1,0:T(8,128)(2,1)S(1)}, u32[]{:S(2)}, u32[]{:S(2)}) collective-permute-start(bf16[32,128,128]{2,1,0:T(8,128)(2,1)S(1)} %slice.301), channel_id=1, source_target_pairs={{1,0},{2,1},{3,2},{5,4},{6,5},{7,6},{9,8},{10,9},{11,10},{13,12},{... | collective-permute-start | bytes 3145736 | tf_op jit(solution)/shard_map/ppermute | solution.py:958
  61.9 43.5 %collective-permute-start.9 = (bf16[64,128,128]{2,1,0:T(8,128)(2,1)S(1)}, bf16[64,128,128]{2,1,0:T(8,128)(2,1)S(1)}, u32[]{:S(2)}, u32[]{:S(2)}) collective-permute-start(bf16[64,128,128]{2,1,0:T(8,128)(2,1)S(1)} %slice_dynamic-update-slice_fusion.12), channel_id=1, source_target_pairs={{0,16},{8,24},{16,0},{24,8},{1,17},{9,25},{17,1},{25,9},{2,18},{10... | collective-permute-start | bytes 6291464 | tf_op jit(solution)/shard_map/ppermute | solution.py:950
  62.4 43.2 %collective-permute-start.8 = (bf16[64,128,128]{2,1,0:T(8,128)(2,1)S(1)}, bf16[64,128,128]{2,1,0:T(8,128)(2,1)S(1)}, u32[]{:S(2)}, u32[]{:S(2)}) collective-permute-start(bf16[64,128,128]{2,1,0:T(8,128)(2,1)S(1)} %slice_dynamic-update-slice_fusion.12), channel_id=1, source_target_pairs={{0,8},{8,0},{16,24},{24,16},{1,9},{9,1},{17,25},{25,17},{2,10},{10... | collective-permute-start | bytes 6291464 | tf_op jit(solution)/shard_map/ppermute | solution.py:950
  79.5 22.5 %collective-permute-start.13 = (bf16[32,128,128]{2,1,0:T(8,128)(2,1)S(1)}, bf16[32,128,128]{2,1,0:T(8,128)(2,1)S(1)}, u32[]{:S(2)}, u32[]{:S(2)}) collective-permute-start(bf16[32,128,128]{2,1,0:T(8,128)(2,1)S(1)} %collective-permute-done.12), channel_id=1, source_target_pairs={{1,2},{2,3},{5,6},{6,7},{9,10},{10,11},{13,14},{14,15},{17,18},{18... | collective-permute-start | bytes 3145736 | tf_op jit(solution)/shard_map/ppermute | solution.py:963
  110.1 21.6 %collective-permute-start.15 = (bf16[32,128,128]{2,1,0:T(8,128)(2,1)S(1)}, bf16[32,128,128]{2,1,0:T(8,128)(2,1)S(1)}, u32[]{:S(2)}, u32[]{:S(2)}) collective-permute-start(bf16[32,128,128]{2,1,0:T(8,128)(2,1)S(1)} %slice.310), channel_id=1, source_target_pairs={{0,8},{8,0},{16,24},{24,16},{1,9},{9,1},{17,25},{25,17},{2,10},{10... | collective-permute-start | bytes 3145736 | tf_op jit(solution)/shard_map/ppermute | solution.py:950
  132.8 87.5 %collective-permute-start.18 = (bf16[128,128,128]{2,1,0:T(8,128)(2,1)}, bf16[128,128,128]{2,1,0:T(8,128)(2,1)}, u32[]{:S(2)}, u32[]{:S(2)}) collective-permute-start(bf16[128,128,128]{2,1,0:T(8,128)(2,1)} %slice_dynamic-update-slice_fusion.4), channel_id=1, source_target_pairs={{0,16},{8,24},{16,0},{24,8},{1,17},{9,25},{17,1},{25,9},{2,18},{10... | collective-permute-start | bytes 12582920 | tf_op jit(solution)/shard_map/ppermute | solution.py:950
  134.4 86.0 %collective-permute-start.17 = (bf16[128,128,128]{2,1,0:T(8,128)(2,1)}, bf16[128,128,128]{2,1,0:T(8,128)(2,1)}, u32[]{:S(2)}, u32[]{:S(2)}) collective-permute-start(bf16[128,128,128]{2,1,0:T(8,128)(2,1)} %slice_dynamic-update-slice_fusion.4), channel_id=1, source_target_pairs={{0,8},{8,0},{16,24},{24,16},{1,9},{9,1},{17,25},{25,17},{2,10},{10... | collective-permute-start | bytes 12582920 | tf_op jit(solution)/shard_map/ppermute | solution.py:950
  134.8 37.3 %collective-permute-start.21 = (bf16[52,128,128]{2,1,0:T(8,128)(2,1)S(1)}, bf16[52,128,128]{2,1,0:T(8,128)(2,1)S(1)}, u32[]{:S(2)}, u32[]{:S(2)}) collective-permute-start(bf16[52,128,128]{2,1,0:T(8,128)(2,1)S(1)} %pad_maximum_fusion.8), channel_id=1, source_target_pairs={{0,1},{1,2},{2,3},{4,5},{5,6},{6,7},{8,9},{9,10},{10,11},{12,13},{... | collective-permute-start | bytes 5111816 | tf_op jit(solution)/shard_map/ppermute | solution.py:958
  139.1 37.3 %collective-permute-start.19 = (bf16[52,128,128]{2,1,0:T(8,128)(2,1)S(1)}, bf16[52,128,128]{2,1,0:T(8,128)(2,1)S(1)}, u32[]{:S(2)}, u32[]{:S(2)}) collective-permute-start(bf16[52,128,128]{2,1,0:T(8,128)(2,1)S(1)} %pad_maximum_fusion.8), channel_id=1, source_target_pairs={{1,0},{2,1},{3,2},{5,4},{6,5},{7,6},{9,8},{10,9},{11,10},{13,12},{... | collective-permute-start | bytes 5111816 | tf_op jit(solution)/shard_map/ppermute | solution.py:958
  172.0 32.8 %collective-permute-start.22 = (bf16[52,128,128]{2,1,0:T(8,128)(2,1)S(1)}, bf16[52,128,128]{2,1,0:T(8,128)(2,1)S(1)}, u32[]{:S(2)}, u32[]{:S(2)}) collective-permute-start(bf16[52,128,128]{2,1,0:T(8,128)(2,1)S(1)} %collective-permute-done.21), channel_id=1, source_target_pairs={{1,2},{2,3},{5,6},{6,7},{9,10},{10,11},{13,14},{14,15},{17,18},{18... | collective-permute-start | bytes 5111816 | tf_op jit(solution)/shard_map/ppermute | solution.py:963
  176.4 30.3 %collective-permute-start.20 = (bf16[52,128,128]{2,1,0:T(8,128)(2,1)S(1)}, bf16[52,128,128]{2,1,0:T(8,128)(2,1)S(1)}, u32[]{:S(2)}, u32[]{:S(2)}) collective-permute-start(bf16[52,128,128]{2,1,0:T(8,128)(2,1)S(1)} %collective-permute-done.19), channel_id=1, source_target_pairs={{1,0},{2,1},{5,4},{6,5},{9,8},{10,9},{13,12},{14,13},{17,16},{18,1... | collective-permute-start | bytes 5111816 | tf_op jit(solution)/shard_map/ppermute | solution.py:962
  220.3 56.9 %collective-permute-start.26 = (bf16[256,128,128]{2,1,0:T(8,128)(2,1)}, bf16[256,128,128]{2,1,0:T(8,128)(2,1)}, u32[]{:S(2)}, u32[]{:S(2)}) collective-permute-start(bf16[256,128,128]{2,1,0:T(8,128)(2,1)} %constant_dynamic-update-slice_fusion), channel_id=1, source_target_pairs={{0,4},{4,0},{1,5},{5,1},{2,6},{6,2},{3,7},{7,3},{8,12},{12,8},{9,1... | collective-permute-start | bytes 25165832 | tf_op jit(solution)/shard_map/ppermute | solution.py:946
  226.6 48.4 %collective-permute-start.24 = (bf16[64,128,128]{2,1,0:T(8,128)(2,1)}, bf16[64,128,128]{2,1,0:T(8,128)(2,1)}, u32[]{:S(2)}, u32[]{:S(2)}) collective-permute-start(bf16[64,128,128]{2,1,0:T(8,128)(2,1)} %slice.313), channel_id=1, source_target_pairs={{0,16},{8,24},{16,0},{24,8},{1,17},{9,25},{17,1},{25,9},{2,18},{10... | collective-permute-start | bytes 6291464 | tf_op jit(solution)/shard_map/ppermute | solution.py:950
  228.1 48.1 %collective-permute-start.23 = (bf16[64,128,128]{2,1,0:T(8,128)(2,1)}, bf16[64,128,128]{2,1,0:T(8,128)(2,1)}, u32[]{:S(2)}, u32[]{:S(2)}) collective-permute-start(bf16[64,128,128]{2,1,0:T(8,128)(2,1)} %slice.312), channel_id=1, source_target_pairs={{0,8},{8,0},{16,24},{24,16},{1,9},{9,1},{17,25},{25,17},{2,10},{10... | collective-permute-start | bytes 6291464 | tf_op jit(solution)/shard_map/ppermute | solution.py:950
  228.6 39.6 %collective-permute-start.25 = (bf16[52,128,128]{2,1,0:T(8,128)(2,1)S(1)}, bf16[52,128,128]{2,1,0:T(8,128)(2,1)}, u32[]{:S(2)}, u32[]{:S(2)}) collective-permute-start(bf16[52,128,128]{2,1,0:T(8,128)(2,1)S(1)} %broadcast_select_fusion.3), channel_id=1, source_target_pairs={{1,0},{2,3},{5,4},{6,7},{9,8},{10,11},{13,12},{14,15},{17,16},{18,... | collective-permute-start | bytes 5111816 | tf_op jit(solution)/shard_map/ppermute | solution.py:968
  276.2 25.6 %collective-permute-start.27 = (bf16[128,128,128]{2,1,0:T(8,128)(2,1)}, bf16[128,128,128]{2,1,0:T(8,128)(2,1)}, u32[]{:S(2)}, u32[]{:S(2)}) collective-permute-start(bf16[128,128,128]{2,1,0:T(8,128)(2,1)} %slice_dynamic-update-slice_fusion.4), channel_id=1, source_target_pairs={{0,4},{4,0},{1,5},{5,1},{2,6},{6,2},{3,7},{7,3},{8,12},{12,8},{9,1... | collective-permute-start | bytes 12582920 | tf_op jit(solution)/shard_map/ppermute | solution.py:946
  276.2 30.5 %collective-permute-start.28 = (bf16[128,128,128]{2,1,0:T(8,128)(2,1)}, bf16[128,128,128]{2,1,0:T(8,128)(2,1)}, u32[]{:S(2)}, u32[]{:S(2)}) collective-permute-start(bf16[128,128,128]{2,1,0:T(8,128)(2,1)} %collective-permute-done.17), channel_id=1, source_target_pairs={{0,4},{4,0},{1,5},{5,1},{2,6},{6,2},{3,7},{7,3},{8,12},{12,8},{9,1... | collective-permute-start | bytes 12582920 | tf_op jit(solution)/shard_map/ppermute | solution.py:946
  276.7 34.7 %collective-permute-start.29 = (bf16[128,128,128]{2,1,0:T(8,128)(2,1)}, bf16[128,128,128]{2,1,0:T(8,128)(2,1)}, u32[]{:S(2)}, u32[]{:S(2)}) collective-permute-start(bf16[128,128,128]{2,1,0:T(8,128)(2,1)} %collective-permute-done.18), channel_id=1, source_target_pairs={{0,4},{4,0},{1,5},{5,1},{2,6},{6,2},{3,7},{7,3},{8,12},{12,8},{9,1... | collective-permute-start | bytes 12582920 | tf_op jit(solution)/shard_map/ppermute | solution.py:946
  276.7 39.5 %collective-permute-start.30 = (bf16[64,128,128]{2,1,0:T(8,128)(2,1)}, bf16[64,128,128]{2,1,0:T(8,128)(2,1)}, u32[]{:S(2)}, u32[]{:S(2)}) collective-permute-start(bf16[64,128,128]{2,1,0:T(8,128)(2,1)} %collective-permute-done.23), channel_id=1, source_target_pairs={{0,4},{4,0},{1,5},{5,1},{2,6},{6,2},{3,7},{7,3},{8,12},{12,8},{9,1... | collective-permute-start | bytes 6291464 | tf_op jit(solution)/shard_map/ppermute | solution.py:946
  277.2 42.2 %collective-permute-start.31 = (bf16[64,128,128]{2,1,0:T(8,128)(2,1)}, bf16[64,128,128]{2,1,0:T(8,128)(2,1)}, u32[]{:S(2)}, u32[]{:S(2)}) collective-permute-start(bf16[64,128,128]{2,1,0:T(8,128)(2,1)} %collective-permute-done.24), channel_id=1, source_target_pairs={{0,4},{4,0},{1,5},{5,1},{2,6},{6,2},{3,7},{7,3},{8,12},{12,8},{9,1... | collective-permute-start | bytes 6291464 | tf_op jit(solution)/shard_map/ppermute | solution.py:946
  279.2 74.9 %all-to-all-start = ((bf16[32,32,1536]{2,1,0:T(8,128)(2,1)}), bf16[32,32,1536]{2,1,0:T(8,128)(2,1)}, u32[]{:S(2)}, u32[]{:S(2)}) async-start(bf16[32,32,1536]{2,1,0:T(8,128)(2,1)} %bitcast.74), calls=%async_computation | async-start | bytes 6291456 | tf_op jit(solution)/shard_map/all_to_all | solution.py:1054
  301.8 28.2 %collective-permute-start.32 = (bf16[104,128,128]{2,1,0:T(8,128)(2,1)S(1)}, bf16[104,128,128]{2,1,0:T(8,128)(2,1)S(1)}, u32[]{:S(2)}, u32[]{:S(2)}) collective-permute-start(bf16[104,128,128]{2,1,0:T(8,128)(2,1)S(1)} %copy-done.8), channel_id=1, source_target_pairs={{0,4},{4,0},{1,5},{5,1},{2,6},{6,2},{3,7},{7,3},{8,12},{12,8},{9,1... | collective-permute-start | bytes 10223624 | tf_op jit(solution)/shard_map/ppermute | solution.py:946
  358.5 82.5 %all-to-all-start.1 = ((bf16[32,32,1536]{2,1,0:T(8,128)(2,1)}), bf16[32,32,1536]{2,1,0:T(8,128)(2,1)S(1)}, u32[]{:S(2)}, u32[]{:S(2)}) async-start(bf16[32,32,1536]{2,1,0:T(8,128)(2,1)} %gather_fusion.1), calls=%async_computation.1 | async-start | bytes 6291456 | tf_op jit(solution)/shard_map/all_to_all | solution.py:1256
  717.0 21.8 %collective-permute-start.35 = (bf16[384,128,128]{2,1,0:T(8,128)(2,1)S(1)}, bf16[384,128,128]{2,1,0:T(8,128)(2,1)}, u32[]{:S(2)}, u32[]{:S(2)}) collective-permute-start(bf16[384,128,128]{2,1,0:T(8,128)(2,1)S(1)} %slice.393), channel_id=1, source_target_pairs={{0,4},{4,0},{1,5},{5,1},{2,6},{6,2},{3,7},{7,3},{8,12},{12,8},{9,1... | collective-permute-start | bytes 37748744 | tf_op jit(solution)/shard_map/ppermute | solution.py:946
  738.8 26.8 %collective-permute-start.46 = (bf16[208,128,128]{2,1,0:T(8,128)(2,1)}, bf16[208,128,128]{2,1,0:T(8,128)(2,1)}, u32[]{:S(2)}, u32[]{:S(2)}) collective-permute-start(bf16[208,128,128]{2,1,0:T(8,128)(2,1)} %slice.396), channel_id=1, source_target_pairs={{0,4},{4,0},{1,5},{5,1},{2,6},{6,2},{3,7},{7,3},{8,12},{12,8},{9,1... | collective-permute-start | bytes 20447240 | tf_op jit(solution)/shard_map/ppermute | solution.py:946
  739.0 62.1 %collective-permute-start.38 = (bf16[192,128,128]{2,1,0:T(8,128)(2,1)}, bf16[192,128,128]{2,1,0:T(8,128)(2,1)}, u32[]{:S(2)}, u32[]{:S(2)}) collective-permute-start(bf16[192,128,128]{2,1,0:T(8,128)(2,1)} %slice.394), channel_id=1, source_target_pairs={{0,4},{4,0},{1,5},{5,1},{2,6},{6,2},{3,7},{7,3},{8,12},{12,8},{9,1... | collective-permute-start | bytes 18874376 | tf_op jit(solution)/shard_map/ppermute | solution.py:946
  746.9 48.0 %collective-permute-start.37 = (bf16[64,128,128]{2,1,0:T(8,128)(2,1)}, bf16[64,128,128]{2,1,0:T(8,128)(2,1)}, u32[]{:S(2)}, u32[]{:S(2)}) collective-permute-start(bf16[64,128,128]{2,1,0:T(8,128)(2,1)} %get-tuple-element.194), channel_id=1, source_target_pairs={{0,8},{8,0},{16,24},{24,16},{1,9},{9,1},{17,25},{25,17},{2,10},{10... | collective-permute-start | bytes 6291464 | tf_op jit(solution)/shard_map/ppermute | solution.py:950
  748.3 47.7 %collective-permute-start.36 = (bf16[64,128,128]{2,1,0:T(8,128)(2,1)}, bf16[64,128,128]{2,1,0:T(8,128)(2,1)}, u32[]{:S(2)}, u32[]{:S(2)}) collective-permute-start(bf16[64,128,128]{2,1,0:T(8,128)(2,1)} %get-tuple-element.195), channel_id=1, source_target_pairs={{0,16},{8,24},{16,0},{24,8},{1,17},{9,25},{17,1},{25,9},{2,18},{10... | collective-permute-start | bytes 6291464 | tf_op jit(solution)/shard_map/ppermute | solution.py:950
  749.8 51.2 %collective-permute-start.39 = (bf16[64,128,128]{2,1,0:T(8,128)(2,1)}, bf16[64,128,128]{2,1,0:T(8,128)(2,1)}, u32[]{:S(2)}, u32[]{:S(2)}) collective-permute-start(bf16[64,128,128]{2,1,0:T(8,128)(2,1)} %slice.395), channel_id=1, source_target_pairs={{0,4},{4,0},{1,5},{5,1},{2,6},{6,2},{3,7},{7,3},{8,12},{12,8},{9,1... | collective-permute-start | bytes 6291464 | tf_op jit(solution)/shard_map/ppermute | solution.py:946
  781.4 41.7 %collective-permute-start.47 = (bf16[52,128,128]{2,1,0:T(8,128)(2,1)}, bf16[52,128,128]{2,1,0:T(8,128)(2,1)S(1)}, u32[]{:S(2)}, u32[]{:S(2)}) collective-permute-start(bf16[52,128,128]{2,1,0:T(8,128)(2,1)} %broadcast_select_fusion), channel_id=1, source_target_pairs={{0,1},{3,2},{4,5},{7,6},{8,9},{11,10},{12,13},{15,14},{16,17},{19,... | collective-permute-start | bytes 5111816 | tf_op jit(solution)/shard_map/ppermute | solution.py:1076
  801.0 91.6 %collective-permute-start.44 = (bf16[2,64,128,128]{3,2,1,0:T(8,128)(2,1)S(1)}, bf16[2,64,128,128]{3,2,1,0:T(8,128)(2,1)S(1)}, u32[]{:S(2)}, u32[]{:S(2)}) collective-permute-start(bf16[2,64,128,128]{3,2,1,0:T(8,128)(2,1)S(1)} %pad_maximum_fusion), channel_id=1, source_target_pairs={{0,8},{8,0},{16,24},{24,16},{1,9},{9,1},{17,25},{25,17},{2,10},{10... | collective-permute-start | bytes 12582920 | tf_op jit(solution)/shard_map/ppermute | solution.py:950
  801.7 93.7 %collective-permute-start.45 = (bf16[2,64,128,128]{3,2,1,0:T(8,128)(2,1)S(1)}, bf16[2,64,128,128]{3,2,1,0:T(8,128)(2,1)}, u32[]{:S(2)}, u32[]{:S(2)}) collective-permute-start(bf16[2,64,128,128]{3,2,1,0:T(8,128)(2,1)S(1)} %pad_maximum_fusion.1), channel_id=1, source_target_pairs={{0,16},{8,24},{16,0},{24,8},{1,17},{9,25},{17,1},{25,9},{2,18},{10... | collective-permute-start | bytes 12582920 | tf_op jit(solution)/shard_map/ppermute | solution.py:950
  823.7 40.8 %collective-permute-start.50 = (bf16[52,128,128]{2,1,0:T(8,128)(2,1)S(1)}, bf16[52,128,128]{2,1,0:T(8,128)(2,1)S(1)}, u32[]{:S(2)}, u32[]{:S(2)}) collective-permute-start(bf16[52,128,128]{2,1,0:T(8,128)(2,1)S(1)} %add_convert_fusion.11), channel_id=1, source_target_pairs={{2,1},{3,2},{6,5},{7,6},{10,9},{11,10},{14,13},{15,14},{18,17},{19... | collective-permute-start | bytes 5111816 | tf_op jit(solution)/shard_map/ppermute | solution.py:1083
  826.1 40.6 %collective-permute-start.48 = (bf16[52,128,128]{2,1,0:T(8,128)(2,1)S(1)}, bf16[52,128,128]{2,1,0:T(8,128)(2,1)S(1)}, u32[]{:S(2)}, u32[]{:S(2)}) collective-permute-start(bf16[52,128,128]{2,1,0:T(8,128)(2,1)S(1)} %add_convert_fusion.11), channel_id=1, source_target_pairs={{0,1},{1,2},{4,5},{5,6},{8,9},{9,10},{12,13},{13,14},{16,17},{17,1... | collective-permute-start | bytes 5111816 | tf_op jit(solution)/shard_map/ppermute | solution.py:1082
  868.2 39.9 %collective-permute-start.49 = (bf16[52,128,128]{2,1,0:T(8,128)(2,1)S(1)}, bf16[52,128,128]{2,1,0:T(8,128)(2,1)}, u32[]{:S(2)}, u32[]{:S(2)}) collective-permute-start(bf16[52,128,128]{2,1,0:T(8,128)(2,1)S(1)} %get-tuple-element.186), channel_id=1, source_target_pairs={{0,1},{1,2},{2,3},{4,5},{5,6},{6,7},{8,9},{9,10},{10,11},{12,13},{... | collective-permute-start | bytes 5111816 | tf_op jit(solution)/shard_map/ppermute | solution.py:1089
  870.1 40.1 %collective-permute-start.51 = (bf16[52,128,128]{2,1,0:T(8,128)(2,1)S(1)}, bf16[52,128,128]{2,1,0:T(8,128)(2,1)}, u32[]{:S(2)}, u32[]{:S(2)}) collective-permute-start(bf16[52,128,128]{2,1,0:T(8,128)(2,1)S(1)} %get-tuple-element.187), channel_id=1, source_target_pairs={{1,0},{2,1},{3,2},{5,4},{6,5},{7,6},{9,8},{10,9},{11,10},{13,12},{... | collective-permute-start | bytes 5111816 | tf_op jit(solution)/shard_map/ppermute | solution.py:1090
  878.8 45.8 %collective-permute-start.40 = (bf16[32,128,128]{2,1,0:T(8,128)(2,1)}, bf16[32,128,128]{2,1,0:T(8,128)(2,1)}, u32[]{:S(2)}, u32[]{:S(2)}) collective-permute-start(bf16[32,128,128]{2,1,0:T(8,128)(2,1)} %get-tuple-element.198), channel_id=1, source_target_pairs={{0,16},{8,24},{16,0},{24,8},{1,17},{9,25},{17,1},{25,9},{2,18},{10... | collective-permute-start | bytes 3145736 | tf_op jit(solution)/shard_map/ppermute | solution.py:950
  894.7 29.8 %collective-permute-start.42 = (bf16[32,128,128]{2,1,0:T(8,128)(2,1)}, bf16[32,128,128]{2,1,0:T(8,128)(2,1)}, u32[]{:S(2)}, u32[]{:S(2)}) collective-permute-start(bf16[32,128,128]{2,1,0:T(8,128)(2,1)} %get-tuple-element.199), channel_id=1, source_target_pairs={{0,8},{8,0},{16,24},{24,16},{1,9},{9,1},{17,25},{25,17},{2,10},{10... | collective-permute-start | bytes 3145736 | tf_op jit(solution)/shard_map/ppermute | solution.py:950
  915.4 25.1 %collective-permute-start.52 = (bf16[32,128,128]{2,1,0:T(8,128)(2,1)}, bf16[32,128,128]{2,1,0:T(8,128)(2,1)}, u32[]{:S(2)}, u32[]{:S(2)}) collective-permute-start(bf16[32,128,128]{2,1,0:T(8,128)(2,1)} %broadcast_select_fusion.4), channel_id=1, source_target_pairs={{0,1},{3,2},{4,5},{7,6},{8,9},{11,10},{12,13},{15,14},{16,17},{19,... | collective-permute-start | bytes 3145736 | tf_op jit(solution)/shard_map/ppermute | solution.py:1076
  927.1 49.8 %collective-permute-start.43 = (bf16[2,32,128,128]{3,2,1,0:T(8,128)(2,1)S(1)}, bf16[2,32,128,128]{3,2,1,0:T(8,128)(2,1)S(1)}, u32[]{:S(2)}, u32[]{:S(2)}) collective-permute-start(bf16[2,32,128,128]{3,2,1,0:T(8,128)(2,1)S(1)} %pad_maximum_fusion.5), channel_id=1, source_target_pairs={{0,16},{8,24},{16,0},{24,8},{1,17},{9,25},{17,1},{25,9},{2,18},{10... | collective-permute-start | bytes 6291464 | tf_op jit(solution)/shard_map/ppermute | solution.py:950
  927.9 49.0 %collective-permute-start.41 = (bf16[2,32,128,128]{3,2,1,0:T(8,128)(2,1)S(1)}, bf16[2,32,128,128]{3,2,1,0:T(8,128)(2,1)S(1)}, u32[]{:S(2)}, u32[]{:S(2)}) collective-permute-start(bf16[2,32,128,128]{3,2,1,0:T(8,128)(2,1)S(1)} %pad_maximum_fusion.4), channel_id=1, source_target_pairs={{0,8},{8,0},{16,24},{24,16},{1,9},{9,1},{17,25},{25,17},{2,10},{10... | collective-permute-start | bytes 6291464 | tf_op jit(solution)/shard_map/ppermute | solution.py:950
  942.1 24.0 %collective-permute-start.55 = (bf16[32,128,128]{2,1,0:T(8,128)(2,1)S(1)}, bf16[32,128,128]{2,1,0:T(8,128)(2,1)S(1)}, u32[]{:S(2)}, u32[]{:S(2)}) collective-permute-start(bf16[32,128,128]{2,1,0:T(8,128)(2,1)S(1)} %add_convert_fusion.14), channel_id=1, source_target_pairs={{2,1},{3,2},{6,5},{7,6},{10,9},{11,10},{14,13},{15,14},{18,17},{19... | collective-permute-start | bytes 3145736 | tf_op jit(solution)/shard_map/ppermute | solution.py:1083
  945.6 23.3 %collective-permute-start.53 = (bf16[32,128,128]{2,1,0:T(8,128)(2,1)S(1)}, bf16[32,128,128]{2,1,0:T(8,128)(2,1)S(1)}, u32[]{:S(2)}, u32[]{:S(2)}) collective-permute-start(bf16[32,128,128]{2,1,0:T(8,128)(2,1)S(1)} %add_convert_fusion.14), channel_id=1, source_target_pairs={{0,1},{1,2},{4,5},{5,6},{8,9},{9,10},{12,13},{13,14},{16,17},{17,1... | collective-permute-start | bytes 3145736 | tf_op jit(solution)/shard_map/ppermute | solution.py:1082
  970.0 22.4 %collective-permute-start.54 = (bf16[32,128,128]{2,1,0:T(8,128)(2,1)S(1)}, bf16[32,128,128]{2,1,0:T(8,128)(2,1)S(1)}, u32[]{:S(2)}, u32[]{:S(2)}) collective-permute-start(bf16[32,128,128]{2,1,0:T(8,128)(2,1)S(1)} %get-tuple-element.192), channel_id=1, source_target_pairs={{0,1},{1,2},{2,3},{4,5},{5,6},{6,7},{8,9},{9,10},{10,11},{12,13},{... | collective-permute-start | bytes 3145736 | tf_op jit(solution)/shard_map/ppermute | solution.py:1089
  972.0 22.7 %collective-permute-start.56 = (bf16[32,128,128]{2,1,0:T(8,128)(2,1)S(1)}, bf16[32,128,128]{2,1,0:T(8,128)(2,1)S(1)}, u32[]{:S(2)}, u32[]{:S(2)}) collective-permute-start(bf16[32,128,128]{2,1,0:T(8,128)(2,1)S(1)} %get-tuple-element.193), channel_id=1, source_target_pairs={{1,0},{2,1},{3,2},{5,4},{6,5},{7,6},{9,8},{10,9},{11,10},{13,12},{... | collective-permute-start | bytes 3145736 | tf_op jit(solution)/shard_map/ppermute | solution.py:1090
  1026.6 24.8 %collective-permute-start.59 = (bf16[16,128,128]{2,1,0:T(8,128)(2,1)S(1)}, bf16[16,128,128]{2,1,0:T(8,128)(2,1)S(1)}, u32[]{:S(2)}, u32[]{:S(2)}) collective-permute-start(bf16[16,128,128]{2,1,0:T(8,128)(2,1)S(1)} %get-tuple-element.196), channel_id=1, source_target_pairs={{0,1},{1,2},{2,3},{4,5},{5,6},{6,7},{8,9},{9,10},{10,11},{12,13},{... | collective-permute-start | bytes 1572872 | tf_op jit(solution)/shard_map/ppermute | solution.py:1089
  1028.5 22.9 %collective-permute-start.61 = (bf16[16,128,128]{2,1,0:T(8,128)(2,1)S(1)}, bf16[16,128,128]{2,1,0:T(8,128)(2,1)S(1)}, u32[]{:S(2)}, u32[]{:S(2)}) collective-permute-start(bf16[16,128,128]{2,1,0:T(8,128)(2,1)S(1)} %get-tuple-element.197), channel_id=1, source_target_pairs={{1,0},{2,1},{3,2},{5,4},{6,5},{7,6},{9,8},{10,9},{11,10},{13,12},{... | collective-permute-start | bytes 1572872 | tf_op jit(solution)/shard_map/ppermute | solution.py:1090
  (48 other events, 747.2 us)

commit v2 on v1

--- a/solution.py
+++ b/solution.py
@@ -42,7 +42,7 @@
 WIDE = BLOCK // E
 FFN_BLOCK = 256
 FFN_WIDE = FFN_BLOCK // E
-CHUNK = 32
+CHUNK = 16
 ROWS = 256
 HIGH_ROWS = 512
 
@@ -214,7 +214,7 @@
         conv_low[pl.ds(r, CHUNK), :] = conv_chunk(branch, r, values[0:4], values[4:5]).astype(BF)
         return 0
 
-    lax.fori_loop(0, length // CHUNK, convolve, 0, unroll=2)
+    lax.fori_loop(0, length // CHUNK, convolve, 0, unroll=4)
     for h in range(WIDE):
         pre[:, h * 2 * E : (h + 1) * 2 * E] = mm(conv_low[:, h * E : (h + 1) * E], wri[slot, h])
 
@@ -245,7 +245,7 @@
         p_out[rows, :] = u * ((1.0 - recall) * values[7:8])
         return carry_out
 
-    lax.fori_loop(0, length // CHUNK, recur, jnp.zeros((1, BLOCK), F32), unroll=2)
+    lax.fori_loop(0, length // CHUNK, recur, jnp.zeros((1, BLOCK), F32), unroll=4)
 
     for c in range(D // ROWS):
         cols = slice(c * ROWS, (c + 1) * ROWS)
@@ -547,7 +547,7 @@
         out.append(sums[KW] + fold(back))
         return tuple(out)
 
-    sums = lax.fori_loop(0, chunks, unconvolve, (eight,) * (KW + 1), unroll=2)
+    sums = lax.fori_loop(0, chunks, unconvolve, (eight,) * (KW + 1), unroll=4)
     for k in range(KW + 1):
         small_grad[k : k + 1, :] = jnp.sum(sums[k], axis=0, keepdims=True)
 

time: 1150 us -> 1150 us (level)
  no operation moved by 1% of the time
where the time goes in v2:
time: 1150 us; the launch traced here: 1130 us
  Pallas kernels  433 us (38%)
  waiting for transfers between devices  325 us (28%)
  local copies, waits for them, and re-layouts  154 us (13%)
  starting transfers between devices  121 us (11%)
  other arithmetic  99 us (9%)
    pallas_call x1, Pallas kernels, ffn(): pl.pallas_call(ffn_kernel, grid_spec=pltpu.PrefetchScalarGridSpec(num_sca...  167 us
    pallas_call x1, Pallas kernels, temporal_backward(): pl.pallas_call(temporal_backward_kernel, grid_spec=pltpu.PrefetchScalarGr...  91.5 us
    pallas_call x1, Pallas kernels, temporal_forward(): pl.pallas_call(temporal_forward_kernel, grid_spec=pltpu.PrefetchScalarGri...  72.3 us
    dynamic_update_slice x18, local copies, waits for them, and re-layouts, put(): buffer = lax.dynamic_update_slice(buffer, piece, (at, 0, 0))  70.6 us
    pallas_call x1, Pallas kernels, solve(): pl.pallas_call(solve_kernel, out_shape=[shape, shape], in_specs=[vmem, vm...  66.3 us
    ppermute x22, waiting for transfers between devices, to_chip(): return lax.ppermute(x, 'yx', swap_pairs(chips, bit))  63.8 us
    ppermute x3, waiting for transfers between devices, fold_two(): from_right = lax.ppermute(middle, 'owner', LEFT[1:])  63 us
    convert_element_type x12, other arithmetic, add_low(): return (a.astype(F32) + b.astype(F32)).astype(BF)  49.4 us
  transfers between devices with their start and end apart: 67, of which 39 were waited for; matrix products, arithmetic and copies ran while one was open for 20% of the time, Pallas kernels for 8%

profile of v2, /device:TPU:16, one launch (start us, length us, event | category | flops | bytes accessed | tf_op | source)
XLA Modules:
  0.0 1134.5 jit_solution(3843765589693776863)
XLA Ops:
  15.7 8.0 collective-permute-done.4
  45.6 6.6 collective-permute-done.7
  63.9 15.5 %collective-permute-done.12 = bf16[32,128,128]{2,1,0:T(8,128)(2,1)S(1)} collective-permute-done((bf16[32,128,128]{2,1,0:T(8,128)(2,1)S(1)}, bf16[32,128,128]{2,1,0:T(8,128)(2,1)S(1)}, u32[]{:S(2)}, u32[]{:S(2)}) %collective-permute-start.12) | collective-permute-done | bytes 1048608 | tf_op jit(solution)/shard_map/ppermute | solution.py:958
  85.5 16.5 %collective-permute-done.13 = bf16[32,128,128]{2,1,0:T(8,128)(2,1)S(1)} collective-permute-done((bf16[32,128,128]{2,1,0:T(8,128)(2,1)S(1)}, bf16[32,128,128]{2,1,0:T(8,128)(2,1)S(1)}, u32[]{:S(2)}, u32[]{:S(2)}) %collective-permute-start.13) | collective-permute-done | bytes 1048608 | tf_op jit(solution)/shard_map/ppermute | solution.py:963
  113.3 12.4 %collective-permute-done.14 = bf16[32,128,128]{2,1,0:T(8,128)(2,1)S(1)} collective-permute-done((bf16[32,128,128]{2,1,0:T(8,128)(2,1)S(1)}, bf16[32,128,128]{2,1,0:T(8,128)(2,1)S(1)}, u32[]{:S(2)}, u32[]{:S(2)}) %collective-permute-start.14) | collective-permute-done | bytes 1048608 | tf_op jit(solution)/shard_map/ppermute | solution.py:968
  134.8 4.4 collective-permute-start.21
  141.1 30.9 %collective-permute-done.21 = bf16[52,128,128]{2,1,0:T(8,128)(2,1)S(1)} collective-permute-done((bf16[52,128,128]{2,1,0:T(8,128)(2,1)S(1)}, bf16[52,128,128]{2,1,0:T(8,128)(2,1)S(1)}, u32[]{:S(2)}, u32[]{:S(2)}) %collective-permute-start.21) | collective-permute-done | bytes 1703968 | tf_op jit(solution)/shard_map/ppermute | solution.py:958
  172.0 4.4 collective-permute-start.22
  185.0 19.8 %collective-permute-done.22 = bf16[52,128,128]{2,1,0:T(8,128)(2,1)S(1)} collective-permute-done((bf16[52,128,128]{2,1,0:T(8,128)(2,1)S(1)}, bf16[52,128,128]{2,1,0:T(8,128)(2,1)S(1)}, u32[]{:S(2)}, u32[]{:S(2)}) %collective-permute-start.22) | collective-permute-done | bytes 1703968 | tf_op jit(solution)/shard_map/ppermute | solution.py:963
  206.9 13.4 %collective-permute-done.18 = bf16[128,128,128]{2,1,0:T(8,128)(2,1)} collective-permute-done((bf16[128,128,128]{2,1,0:T(8,128)(2,1)}, bf16[128,128,128]{2,1,0:T(8,128)(2,1)}, u32[]{:S(2)}, u32[]{:S(2)}) %collective-permute-start.18) | collective-permute-done | bytes 4194336 | tf_op jit(solution)/shard_map/ppermute | solution.py:950
  232.9 10.4 constant_dynamic-update-slice_fusion.20
  243.4 4.8 constant_dynamic-update-slice_fusion.19
  248.1 4.8 constant_dynamic-update-slice_fusion.18
  253.0 4.8 constant_dynamic-update-slice_fusion.17
  257.7 10.5 collective-permute-done.25
  268.3 6.7 collective-permute-done.24
  279.2 5.4 all-to-all-start
  284.6 10.5 constant_dynamic-update-slice_fusion.16
  301.9 4.7 constant_dynamic-update-slice_fusion.13
  306.7 4.7 constant_dynamic-update-slice_fusion.12
  311.4 4.8 constant_dynamic-update-slice_fusion.11
  346.7 7.5 all-to-all-done
  358.5 5.9 all-to-all-start.1
  366.9 72.3 %temporal_forward.1 = (f32[1024,2048]{1,0:T(8,128)}, f32[1024,2048]{1,0:T(8,128)}, f32[1024,2048]{1,0:T(8,128)}, f32[1024,2048]{1,0:T(8,128)}, f32[1024,2048]{1,...) custom-call(s32[1920]{0:T(1024)} %select_reduce_fusion.pos, ...), custom_call_target="tpu_custom_call" | custom-call | flops 19327352832 | bytes 115343360 | tf_op jit(solution)/shard_map/temporal_forward/pallas_call | solution.py:264
  441.4 166.7 %ffn_both_ways.1 = (bf16[1952,128,128]{2,1,0:T(8,128)(2,1)}, bf16[1024,1536]{1,0:T(8,128)(2,1)}, f32[1024,1536]{1,0:T(8,128)}, bf16[1024,1536]{1,0:T(8,128)(2,1)}, f32[1,1536]{1,0:T(1,128)}) custom-call(s32[1920]{0:T(1024)} %select_reduce_fusion.pos, bf16[1952,128,128]{2,1,0:T(8,128)(2,1)} %slice_dynamic-update-slice_fusion.packed, ...), custom_call_target="tpu_custom_call" | custom-call | flops 130459631616 | bytes 115343360 | tf_op jit(solution)/shard_map/ffn_both_ways/pallas_call | solution.py:402
  608.2 91.5 %temporal_backward.1 = (bf16[1952,128,128]{2,1,0:T(8,128)(2,1)}, bf16[1024,1536]{1,0:T(8,128)(2,1)}, f32[1,1536]{1,0:T(1,128)}, f32[8,2048]{1,0:T(8,128)}) custom-call(s32[1920]{0:T(1024)} %select_reduce_fusion.pos, bf16[1952,128,128]{2,1,0:T(8,128)(2,1)} %slice_dynamic-update-slice_fusion.packed, ...), custom_call_target="tpu_custom_call", output_to_operand_aliasing={{0}: (2, {})} | custom-call | flops 38654705664 | bytes 136314880 | tf_op jit(solution)/shard_map/temporal_backward/pallas_call | solution.py:603
  701.7 4.6 scatter_fusion
  709.1 6.7 slice.393
  721.2 8.0 slice.394
  729.2 8.6 slice.396
  738.4 5.3 add_convert_fusion.4
  748.9 15.7 %add_convert_fusion = bf16[384,128,128]{2,1,0:T(8,128)(2,1)} fusion(bf16[384,128,128]{2,1,0:T(8,128)(2,1)} %collective-permute-done.35, bf16[1952,128,128]{2,1,0:T(8,128)(2,1)} %scatter_fusion), kind=kLoop, calls=%fused_computation.3 | loop fusion | flops 25165824 | bytes 37748736 | tf_op jit(solution)/shard_map/convert_element_type | solution.py:942
  764.6 12.5 %add_convert_fusion.1 = bf16[208,128,128]{2,1,0:T(8,128)(2,1)} fusion(bf16[208,128,128]{2,1,0:T(8,128)(2,1)} %collective-permute-done.46, bf16[1952,128,128]{2,1,0:T(8,128)(2,1)} %scatter_fusion), kind=kLoop, calls=%fused_computation.6 | loop fusion | flops 13631488 | bytes 20447232 | tf_op jit(solution)/shard_map/convert_element_type | solution.py:942
  785.1 8.9 collective-permute-done.37
  802.2 19.9 %collective-permute-done.47 = bf16[52,128,128]{2,1,0:T(8,128)(2,1)S(1)} collective-permute-done((bf16[52,128,128]{2,1,0:T(8,128)(2,1)}, bf16[52,128,128]{2,1,0:T(8,128)(2,1)S(1)}, u32[]{:S(2)}, u32[]{:S(2)}) %collective-permute-start.47) | collective-permute-done | bytes 1703968 | tf_op jit(solution)/shard_map/ppermute | solution.py:1076
  826.5 37.1 %collective-permute-done.50 = bf16[52,128,128]{2,1,0:T(8,128)(2,1)S(1)} collective-permute-done((bf16[52,128,128]{2,1,0:T(8,128)(2,1)S(1)}, bf16[52,128,128]{2,1,0:T(8,128)(2,1)S(1)}, u32[]{:S(2)}, u32[]{:S(2)}) %collective-permute-start.50) | collective-permute-done | bytes 1703968 | tf_op jit(solution)/shard_map/ppermute | solution.py:1083
  878.4 13.2 %collective-permute-done.44 = bf16[2,64,128,128]{3,2,1,0:T(8,128)(2,1)S(1)} collective-permute-done((bf16[2,64,128,128]{3,2,1,0:T(8,128)(2,1)S(1)}, bf16[2,64,128,128]{3,2,1,0:T(8,128)(2,1)S(1)}, u32[]{:S(2)}, u32[]{:S(2)}) %collective-permute-start.44) | collective-permute-done | bytes 4194336 | tf_op jit(solution)/shard_map/ppermute | solution.py:950
  894.4 8.3 add_convert_fusion.3
  916.0 7.5 add_convert_fusion.2
  927.7 11.9 %collective-permute-done.52 = bf16[32,128,128]{2,1,0:T(8,128)(2,1)} collective-permute-done((bf16[32,128,128]{2,1,0:T(8,128)(2,1)}, bf16[32,128,128]{2,1,0:T(8,128)(2,1)}, u32[]{:S(2)}, u32[]{:S(2)}) %collective-permute-start.52) | collective-permute-done | bytes 1048608 | tf_op jit(solution)/shard_map/ppermute | solution.py:1076
  946.0 19.2 %collective-permute-done.55 = bf16[32,128,128]{2,1,0:T(8,128)(2,1)S(1)} collective-permute-done((bf16[32,128,128]{2,1,0:T(8,128)(2,1)S(1)}, bf16[32,128,128]{2,1,0:T(8,128)(2,1)S(1)}, u32[]{:S(2)}, u32[]{:S(2)}) %collective-permute-start.55) | collective-permute-done | bytes 1048608 | tf_op jit(solution)/shard_map/ppermute | solution.py:1083
  979.3 7.2 collective-permute-done.63
  995.9 11.5 %collective-permute-done.57 = bf16[16,128,128]{2,1,0:T(8,128)(2,1)S(1)} collective-permute-done((bf16[16,128,128]{2,1,0:T(8,128)(2,1)S(1)}, bf16[16,128,128]{2,1,0:T(8,128)(2,1)S(1)}, u32[]{:S(2)}, u32[]{:S(2)}) %collective-permute-start.57) | collective-permute-done | bytes 524320 | tf_op jit(solution)/shard_map/ppermute | solution.py:1076
  1011.8 6.7 collective-permute-done.60
  1018.6 6.7 collective-permute-done.58
  1031.5 18.9 %rotate.2 = (f32[60,128,128]{2,1,0:T(8,128)}, f32[60,128,128]{2,1,0:T(8,128)}, f32[60,128,128]{2,1,0:T(8,128)}, f32[60,128,128]{2,1,0:T(8,128)}, f32[60,128,128]...) custom-call(f32[32,128,128]{2,1,0:T(8,128)S(1)} %convert_add_fusion.1.own, ...), custom_call_target="tpu_custom_call" | custom-call | flops 32000000000 | bytes 33554432 | tf_op jit(solution)/shard_map/rotate/pallas_call | solution.py:856
  1050.9 16.8 %rotate.3 = (f32[60,128,128]{2,1,0:T(8,128)}, f32[60,128,128]{2,1,0:T(8,128)}, f32[60,128,128]{2,1,0:T(8,128)}, f32[60,128,128]{2,1,0:T(8,128)}, f32[60,128,128]...) custom-call(f32[29,128,128]{2,1,0:T(8,128)S(1)} %pad_maximum_fusion., ...), custom_call_target="tpu_custom_call", output_to_operand_aliasing={{0}: (8, {}), {1}: (9, {}), {2}: (10, {}), {3}: (11, {}), {... | custom-call | flops 28000000000 | bytes 29360128 | tf_op jit(solution)/shard_map/rotate/pallas_call | solution.py:856
  1067.7 66.3 %cholesky_solve.1 = (f32[60,128,128]{2,1,0:T(8,128)}, f32[60,128,128]{2,1,0:T(8,128)}) custom-call(f32[120,128,128]{2,1,0:T(8,128)} %bitcast.83, f32[120,128,128]{2,1,0:T(8,128)} %bitcast.84), custom_call_target="tpu_custom_call" | custom-call | flops 60000002048 | bytes 23592960 | tf_op jit(solution)/shard_map/cholesky_solve/pallas_call | solution.py:763
  (288 shorter events, 262.3 us)
Async XLA Ops:
  54.9 24.6 %collective-permute-start.12 = (bf16[32,128,128]{2,1,0:T(8,128)(2,1)S(1)}, bf16[32,128,128]{2,1,0:T(8,128)(2,1)S(1)}, u32[]{:S(2)}, u32[]{:S(2)}) collective-permute-start(bf16[32,128,128]{2,1,0:T(8,128)(2,1)S(1)} %slice.301), channel_id=1, source_target_pairs={{0,1},{1,2},{2,3},{4,5},{5,6},{6,7},{8,9},{9,10},{10,11},{12,13},{... | collective-permute-start | bytes 3145736 | tf_op jit(solution)/shard_map/ppermute | solution.py:958
  59.2 23.3 %collective-permute-start.10 = (bf16[32,128,128]{2,1,0:T(8,128)(2,1)S(1)}, bf16[32,128,128]{2,1,0:T(8,128)(2,1)S(1)}, u32[]{:S(2)}, u32[]{:S(2)}) collective-permute-start(bf16[32,128,128]{2,1,0:T(8,128)(2,1)S(1)} %slice.301), channel_id=1, source_target_pairs={{1,0},{2,1},{3,2},{5,4},{6,5},{7,6},{9,8},{10,9},{11,10},{13,12},{... | collective-permute-start | bytes 3145736 | tf_op jit(solution)/shard_map/ppermute | solution.py:958
  61.9 43.5 %collective-permute-start.9 = (bf16[64,128,128]{2,1,0:T(8,128)(2,1)S(1)}, bf16[64,128,128]{2,1,0:T(8,128)(2,1)S(1)}, u32[]{:S(2)}, u32[]{:S(2)}) collective-permute-start(bf16[64,128,128]{2,1,0:T(8,128)(2,1)S(1)} %slice_dynamic-update-slice_fusion.12), channel_id=1, source_target_pairs={{0,16},{8,24},{16,0},{24,8},{1,17},{9,25},{17,1},{25,9},{2,18},{10... | collective-permute-start | bytes 6291464 | tf_op jit(solution)/shard_map/ppermute | solution.py:950
  62.4 43.2 %collective-permute-start.8 = (bf16[64,128,128]{2,1,0:T(8,128)(2,1)S(1)}, bf16[64,128,128]{2,1,0:T(8,128)(2,1)S(1)}, u32[]{:S(2)}, u32[]{:S(2)}) collective-permute-start(bf16[64,128,128]{2,1,0:T(8,128)(2,1)S(1)} %slice_dynamic-update-slice_fusion.12), channel_id=1, source_target_pairs={{0,8},{8,0},{16,24},{24,16},{1,9},{9,1},{17,25},{25,17},{2,10},{10... | collective-permute-start | bytes 6291464 | tf_op jit(solution)/shard_map/ppermute | solution.py:950
  79.5 22.5 %collective-permute-start.13 = (bf16[32,128,128]{2,1,0:T(8,128)(2,1)S(1)}, bf16[32,128,128]{2,1,0:T(8,128)(2,1)S(1)}, u32[]{:S(2)}, u32[]{:S(2)}) collective-permute-start(bf16[32,128,128]{2,1,0:T(8,128)(2,1)S(1)} %collective-permute-done.12), channel_id=1, source_target_pairs={{1,2},{2,3},{5,6},{6,7},{9,10},{10,11},{13,14},{14,15},{17,18},{18... | collective-permute-start | bytes 3145736 | tf_op jit(solution)/shard_map/ppermute | solution.py:963
  110.1 21.6 %collective-permute-start.15 = (bf16[32,128,128]{2,1,0:T(8,128)(2,1)S(1)}, bf16[32,128,128]{2,1,0:T(8,128)(2,1)S(1)}, u32[]{:S(2)}, u32[]{:S(2)}) collective-permute-start(bf16[32,128,128]{2,1,0:T(8,128)(2,1)S(1)} %slice.310), channel_id=1, source_target_pairs={{0,8},{8,0},{16,24},{24,16},{1,9},{9,1},{17,25},{25,17},{2,10},{10... | collective-permute-start | bytes 3145736 | tf_op jit(solution)/shard_map/ppermute | solution.py:950
  132.8 87.5 %collective-permute-start.18 = (bf16[128,128,128]{2,1,0:T(8,128)(2,1)}, bf16[128,128,128]{2,1,0:T(8,128)(2,1)}, u32[]{:S(2)}, u32[]{:S(2)}) collective-permute-start(bf16[128,128,128]{2,1,0:T(8,128)(2,1)} %slice_dynamic-update-slice_fusion.4), channel_id=1, source_target_pairs={{0,16},{8,24},{16,0},{24,8},{1,17},{9,25},{17,1},{25,9},{2,18},{10... | collective-permute-start | bytes 12582920 | tf_op jit(solution)/shard_map/ppermute | solution.py:950
  134.4 86.0 %collective-permute-start.17 = (bf16[128,128,128]{2,1,0:T(8,128)(2,1)}, bf16[128,128,128]{2,1,0:T(8,128)(2,1)}, u32[]{:S(2)}, u32[]{:S(2)}) collective-permute-start(bf16[128,128,128]{2,1,0:T(8,128)(2,1)} %slice_dynamic-update-slice_fusion.4), channel_id=1, source_target_pairs={{0,8},{8,0},{16,24},{24,16},{1,9},{9,1},{17,25},{25,17},{2,10},{10... | collective-permute-start | bytes 12582920 | tf_op jit(solution)/shard_map/ppermute | solution.py:950
  134.8 37.3 %collective-permute-start.21 = (bf16[52,128,128]{2,1,0:T(8,128)(2,1)S(1)}, bf16[52,128,128]{2,1,0:T(8,128)(2,1)S(1)}, u32[]{:S(2)}, u32[]{:S(2)}) collective-permute-start(bf16[52,128,128]{2,1,0:T(8,128)(2,1)S(1)} %pad_maximum_fusion.8), channel_id=1, source_target_pairs={{0,1},{1,2},{2,3},{4,5},{5,6},{6,7},{8,9},{9,10},{10,11},{12,13},{... | collective-permute-start | bytes 5111816 | tf_op jit(solution)/shard_map/ppermute | solution.py:958
  139.1 37.3 %collective-permute-start.19 = (bf16[52,128,128]{2,1,0:T(8,128)(2,1)S(1)}, bf16[52,128,128]{2,1,0:T(8,128)(2,1)S(1)}, u32[]{:S(2)}, u32[]{:S(2)}) collective-permute-start(bf16[52,128,128]{2,1,0:T(8,128)(2,1)S(1)} %pad_maximum_fusion.8), channel_id=1, source_target_pairs={{1,0},{2,1},{3,2},{5,4},{6,5},{7,6},{9,8},{10,9},{11,10},{13,12},{... | collective-permute-start | bytes 5111816 | tf_op jit(solution)/shard_map/ppermute | solution.py:958
  172.0 32.8 %collective-permute-start.22 = (bf16[52,128,128]{2,1,0:T(8,128)(2,1)S(1)}, bf16[52,128,128]{2,1,0:T(8,128)(2,1)S(1)}, u32[]{:S(2)}, u32[]{:S(2)}) collective-permute-start(bf16[52,128,128]{2,1,0:T(8,128)(2,1)S(1)} %collective-permute-done.21), channel_id=1, source_target_pairs={{1,2},{2,3},{5,6},{6,7},{9,10},{10,11},{13,14},{14,15},{17,18},{18... | collective-permute-start | bytes 5111816 | tf_op jit(solution)/shard_map/ppermute | solution.py:963
  176.4 30.3 %collective-permute-start.20 = (bf16[52,128,128]{2,1,0:T(8,128)(2,1)S(1)}, bf16[52,128,128]{2,1,0:T(8,128)(2,1)S(1)}, u32[]{:S(2)}, u32[]{:S(2)}) collective-permute-start(bf16[52,128,128]{2,1,0:T(8,128)(2,1)S(1)} %collective-permute-done.19), channel_id=1, source_target_pairs={{1,0},{2,1},{5,4},{6,5},{9,8},{10,9},{13,12},{14,13},{17,16},{18,1... | collective-permute-start | bytes 5111816 | tf_op jit(solution)/shard_map/ppermute | solution.py:962
  220.3 56.9 %collective-permute-start.26 = (bf16[256,128,128]{2,1,0:T(8,128)(2,1)}, bf16[256,128,128]{2,1,0:T(8,128)(2,1)}, u32[]{:S(2)}, u32[]{:S(2)}) collective-permute-start(bf16[256,128,128]{2,1,0:T(8,128)(2,1)} %constant_dynamic-update-slice_fusion), channel_id=1, source_target_pairs={{0,4},{4,0},{1,5},{5,1},{2,6},{6,2},{3,7},{7,3},{8,12},{12,8},{9,1... | collective-permute-start | bytes 25165832 | tf_op jit(solution)/shard_map/ppermute | solution.py:946
  226.6 48.4 %collective-permute-start.24 = (bf16[64,128,128]{2,1,0:T(8,128)(2,1)}, bf16[64,128,128]{2,1,0:T(8,128)(2,1)}, u32[]{:S(2)}, u32[]{:S(2)}) collective-permute-start(bf16[64,128,128]{2,1,0:T(8,128)(2,1)} %slice.313), channel_id=1, source_target_pairs={{0,16},{8,24},{16,0},{24,8},{1,17},{9,25},{17,1},{25,9},{2,18},{10... | collective-permute-start | bytes 6291464 | tf_op jit(solution)/shard_map/ppermute | solution.py:950
  228.1 48.1 %collective-permute-start.23 = (bf16[64,128,128]{2,1,0:T(8,128)(2,1)}, bf16[64,128,128]{2,1,0:T(8,128)(2,1)}, u32[]{:S(2)}, u32[]{:S(2)}) collective-permute-start(bf16[64,128,128]{2,1,0:T(8,128)(2,1)} %slice.312), channel_id=1, source_target_pairs={{0,8},{8,0},{16,24},{24,16},{1,9},{9,1},{17,25},{25,17},{2,10},{10... | collective-permute-start | bytes 6291464 | tf_op jit(solution)/shard_map/ppermute | solution.py:950
  228.6 39.6 %collective-permute-start.25 = (bf16[52,128,128]{2,1,0:T(8,128)(2,1)S(1)}, bf16[52,128,128]{2,1,0:T(8,128)(2,1)}, u32[]{:S(2)}, u32[]{:S(2)}) collective-permute-start(bf16[52,128,128]{2,1,0:T(8,128)(2,1)S(1)} %broadcast_select_fusion.3), channel_id=1, source_target_pairs={{1,0},{2,3},{5,4},{6,7},{9,8},{10,11},{13,12},{14,15},{17,16},{18,... | collective-permute-start | bytes 5111816 | tf_op jit(solution)/shard_map/ppermute | solution.py:968
  276.2 25.6 %collective-permute-start.27 = (bf16[128,128,128]{2,1,0:T(8,128)(2,1)}, bf16[128,128,128]{2,1,0:T(8,128)(2,1)}, u32[]{:S(2)}, u32[]{:S(2)}) collective-permute-start(bf16[128,128,128]{2,1,0:T(8,128)(2,1)} %slice_dynamic-update-slice_fusion.4), channel_id=1, source_target_pairs={{0,4},{4,0},{1,5},{5,1},{2,6},{6,2},{3,7},{7,3},{8,12},{12,8},{9,1... | collective-permute-start | bytes 12582920 | tf_op jit(solution)/shard_map/ppermute | solution.py:946
  276.2 30.5 %collective-permute-start.28 = (bf16[128,128,128]{2,1,0:T(8,128)(2,1)}, bf16[128,128,128]{2,1,0:T(8,128)(2,1)}, u32[]{:S(2)}, u32[]{:S(2)}) collective-permute-start(bf16[128,128,128]{2,1,0:T(8,128)(2,1)} %collective-permute-done.17), channel_id=1, source_target_pairs={{0,4},{4,0},{1,5},{5,1},{2,6},{6,2},{3,7},{7,3},{8,12},{12,8},{9,1... | collective-permute-start | bytes 12582920 | tf_op jit(solution)/shard_map/ppermute | solution.py:946
  276.7 34.7 %collective-permute-start.29 = (bf16[128,128,128]{2,1,0:T(8,128)(2,1)}, bf16[128,128,128]{2,1,0:T(8,128)(2,1)}, u32[]{:S(2)}, u32[]{:S(2)}) collective-permute-start(bf16[128,128,128]{2,1,0:T(8,128)(2,1)} %collective-permute-done.18), channel_id=1, source_target_pairs={{0,4},{4,0},{1,5},{5,1},{2,6},{6,2},{3,7},{7,3},{8,12},{12,8},{9,1... | collective-permute-start | bytes 12582920 | tf_op jit(solution)/shard_map/ppermute | solution.py:946
  276.7 39.5 %collective-permute-start.30 = (bf16[64,128,128]{2,1,0:T(8,128)(2,1)}, bf16[64,128,128]{2,1,0:T(8,128)(2,1)}, u32[]{:S(2)}, u32[]{:S(2)}) collective-permute-start(bf16[64,128,128]{2,1,0:T(8,128)(2,1)} %collective-permute-done.23), channel_id=1, source_target_pairs={{0,4},{4,0},{1,5},{5,1},{2,6},{6,2},{3,7},{7,3},{8,12},{12,8},{9,1... | collective-permute-start | bytes 6291464 | tf_op jit(solution)/shard_map/ppermute | solution.py:946
  277.2 42.2 %collective-permute-start.31 = (bf16[64,128,128]{2,1,0:T(8,128)(2,1)}, bf16[64,128,128]{2,1,0:T(8,128)(2,1)}, u32[]{:S(2)}, u32[]{:S(2)}) collective-permute-start(bf16[64,128,128]{2,1,0:T(8,128)(2,1)} %collective-permute-done.24), channel_id=1, source_target_pairs={{0,4},{4,0},{1,5},{5,1},{2,6},{6,2},{3,7},{7,3},{8,12},{12,8},{9,1... | collective-permute-start | bytes 6291464 | tf_op jit(solution)/shard_map/ppermute | solution.py:946
  279.2 74.9 %all-to-all-start = ((bf16[32,32,1536]{2,1,0:T(8,128)(2,1)}), bf16[32,32,1536]{2,1,0:T(8,128)(2,1)}, u32[]{:S(2)}, u32[]{:S(2)}) async-start(bf16[32,32,1536]{2,1,0:T(8,128)(2,1)} %bitcast.74), calls=%async_computation | async-start | bytes 6291456 | tf_op jit(solution)/shard_map/all_to_all | solution.py:1054
  301.8 28.2 %collective-permute-start.32 = (bf16[104,128,128]{2,1,0:T(8,128)(2,1)S(1)}, bf16[104,128,128]{2,1,0:T(8,128)(2,1)S(1)}, u32[]{:S(2)}, u32[]{:S(2)}) collective-permute-start(bf16[104,128,128]{2,1,0:T(8,128)(2,1)S(1)} %copy-done.8), channel_id=1, source_target_pairs={{0,4},{4,0},{1,5},{5,1},{2,6},{6,2},{3,7},{7,3},{8,12},{12,8},{9,1... | collective-permute-start | bytes 10223624 | tf_op jit(solution)/shard_map/ppermute | solution.py:946
  358.5 80.7 %all-to-all-start.1 = ((bf16[32,32,1536]{2,1,0:T(8,128)(2,1)}), bf16[32,32,1536]{2,1,0:T(8,128)(2,1)S(1)}, u32[]{:S(2)}, u32[]{:S(2)}) async-start(bf16[32,32,1536]{2,1,0:T(8,128)(2,1)} %gather_fusion.1), calls=%async_computation.1 | async-start | bytes 6291456 | tf_op jit(solution)/shard_map/all_to_all | solution.py:1256
  716.1 21.8 %collective-permute-start.35 = (bf16[384,128,128]{2,1,0:T(8,128)(2,1)S(1)}, bf16[384,128,128]{2,1,0:T(8,128)(2,1)}, u32[]{:S(2)}, u32[]{:S(2)}) collective-permute-start(bf16[384,128,128]{2,1,0:T(8,128)(2,1)S(1)} %slice.393), channel_id=1, source_target_pairs={{0,4},{4,0},{1,5},{5,1},{2,6},{6,2},{3,7},{7,3},{8,12},{12,8},{9,1... | collective-permute-start | bytes 37748744 | tf_op jit(solution)/shard_map/ppermute | solution.py:946
  737.9 26.8 %collective-permute-start.46 = (bf16[208,128,128]{2,1,0:T(8,128)(2,1)}, bf16[208,128,128]{2,1,0:T(8,128)(2,1)}, u32[]{:S(2)}, u32[]{:S(2)}) collective-permute-start(bf16[208,128,128]{2,1,0:T(8,128)(2,1)} %slice.396), channel_id=1, source_target_pairs={{0,4},{4,0},{1,5},{5,1},{2,6},{6,2},{3,7},{7,3},{8,12},{12,8},{9,1... | collective-permute-start | bytes 20447240 | tf_op jit(solution)/shard_map/ppermute | solution.py:946
  738.0 62.1 %collective-permute-start.38 = (bf16[192,128,128]{2,1,0:T(8,128)(2,1)}, bf16[192,128,128]{2,1,0:T(8,128)(2,1)}, u32[]{:S(2)}, u32[]{:S(2)}) collective-permute-start(bf16[192,128,128]{2,1,0:T(8,128)(2,1)} %slice.394), channel_id=1, source_target_pairs={{0,4},{4,0},{1,5},{5,1},{2,6},{6,2},{3,7},{7,3},{8,12},{12,8},{9,1... | collective-permute-start | bytes 18874376 | tf_op jit(solution)/shard_map/ppermute | solution.py:946
  746.0 48.0 %collective-permute-start.37 = (bf16[64,128,128]{2,1,0:T(8,128)(2,1)}, bf16[64,128,128]{2,1,0:T(8,128)(2,1)}, u32[]{:S(2)}, u32[]{:S(2)}) collective-permute-start(bf16[64,128,128]{2,1,0:T(8,128)(2,1)} %get-tuple-element.194), channel_id=1, source_target_pairs={{0,8},{8,0},{16,24},{24,16},{1,9},{9,1},{17,25},{25,17},{2,10},{10... | collective-permute-start | bytes 6291464 | tf_op jit(solution)/shard_map/ppermute | solution.py:950
  747.4 47.7 %collective-permute-start.36 = (bf16[64,128,128]{2,1,0:T(8,128)(2,1)}, bf16[64,128,128]{2,1,0:T(8,128)(2,1)}, u32[]{:S(2)}, u32[]{:S(2)}) collective-permute-start(bf16[64,128,128]{2,1,0:T(8,128)(2,1)} %get-tuple-element.195), channel_id=1, source_target_pairs={{0,16},{8,24},{16,0},{24,8},{1,17},{9,25},{17,1},{25,9},{2,18},{10... | collective-permute-start | bytes 6291464 | tf_op jit(solution)/shard_map/ppermute | solution.py:950
  748.9 51.2 %collective-permute-start.39 = (bf16[64,128,128]{2,1,0:T(8,128)(2,1)}, bf16[64,128,128]{2,1,0:T(8,128)(2,1)}, u32[]{:S(2)}, u32[]{:S(2)}) collective-permute-start(bf16[64,128,128]{2,1,0:T(8,128)(2,1)} %slice.395), channel_id=1, source_target_pairs={{0,4},{4,0},{1,5},{5,1},{2,6},{6,2},{3,7},{7,3},{8,12},{12,8},{9,1... | collective-permute-start | bytes 6291464 | tf_op jit(solution)/shard_map/ppermute | solution.py:946
  780.4 41.7 %collective-permute-start.47 = (bf16[52,128,128]{2,1,0:T(8,128)(2,1)}, bf16[52,128,128]{2,1,0:T(8,128)(2,1)S(1)}, u32[]{:S(2)}, u32[]{:S(2)}) collective-permute-start(bf16[52,128,128]{2,1,0:T(8,128)(2,1)} %broadcast_select_fusion), channel_id=1, source_target_pairs={{0,1},{3,2},{4,5},{7,6},{8,9},{11,10},{12,13},{15,14},{16,17},{19,... | collective-permute-start | bytes 5111816 | tf_op jit(solution)/shard_map/ppermute | solution.py:1076
  800.1 91.6 %collective-permute-start.44 = (bf16[2,64,128,128]{3,2,1,0:T(8,128)(2,1)S(1)}, bf16[2,64,128,128]{3,2,1,0:T(8,128)(2,1)S(1)}, u32[]{:S(2)}, u32[]{:S(2)}) collective-permute-start(bf16[2,64,128,128]{3,2,1,0:T(8,128)(2,1)S(1)} %pad_maximum_fusion), channel_id=1, source_target_pairs={{0,8},{8,0},{16,24},{24,16},{1,9},{9,1},{17,25},{25,17},{2,10},{10... | collective-permute-start | bytes 12582920 | tf_op jit(solution)/shard_map/ppermute | solution.py:950
  800.8 93.7 %collective-permute-start.45 = (bf16[2,64,128,128]{3,2,1,0:T(8,128)(2,1)S(1)}, bf16[2,64,128,128]{3,2,1,0:T(8,128)(2,1)}, u32[]{:S(2)}, u32[]{:S(2)}) collective-permute-start(bf16[2,64,128,128]{3,2,1,0:T(8,128)(2,1)S(1)} %pad_maximum_fusion.1), channel_id=1, source_target_pairs={{0,16},{8,24},{16,0},{24,8},{1,17},{9,25},{17,1},{25,9},{2,18},{10... | collective-permute-start | bytes 12582920 | tf_op jit(solution)/shard_map/ppermute | solution.py:950
  822.8 40.8 %collective-permute-start.50 = (bf16[52,128,128]{2,1,0:T(8,128)(2,1)S(1)}, bf16[52,128,128]{2,1,0:T(8,128)(2,1)S(1)}, u32[]{:S(2)}, u32[]{:S(2)}) collective-permute-start(bf16[52,128,128]{2,1,0:T(8,128)(2,1)S(1)} %add_convert_fusion.11), channel_id=1, source_target_pairs={{2,1},{3,2},{6,5},{7,6},{10,9},{11,10},{14,13},{15,14},{18,17},{19... | collective-permute-start | bytes 5111816 | tf_op jit(solution)/shard_map/ppermute | solution.py:1083
  825.2 40.6 %collective-permute-start.48 = (bf16[52,128,128]{2,1,0:T(8,128)(2,1)S(1)}, bf16[52,128,128]{2,1,0:T(8,128)(2,1)S(1)}, u32[]{:S(2)}, u32[]{:S(2)}) collective-permute-start(bf16[52,128,128]{2,1,0:T(8,128)(2,1)S(1)} %add_convert_fusion.11), channel_id=1, source_target_pairs={{0,1},{1,2},{4,5},{5,6},{8,9},{9,10},{12,13},{13,14},{16,17},{17,1... | collective-permute-start | bytes 5111816 | tf_op jit(solution)/shard_map/ppermute | solution.py:1082
  867.3 39.9 %collective-permute-start.49 = (bf16[52,128,128]{2,1,0:T(8,128)(2,1)S(1)}, bf16[52,128,128]{2,1,0:T(8,128)(2,1)}, u32[]{:S(2)}, u32[]{:S(2)}) collective-permute-start(bf16[52,128,128]{2,1,0:T(8,128)(2,1)S(1)} %get-tuple-element.186), channel_id=1, source_target_pairs={{0,1},{1,2},{2,3},{4,5},{5,6},{6,7},{8,9},{9,10},{10,11},{12,13},{... | collective-permute-start | bytes 5111816 | tf_op jit(solution)/shard_map/ppermute | solution.py:1089
  869.2 40.1 %collective-permute-start.51 = (bf16[52,128,128]{2,1,0:T(8,128)(2,1)S(1)}, bf16[52,128,128]{2,1,0:T(8,128)(2,1)}, u32[]{:S(2)}, u32[]{:S(2)}) collective-permute-start(bf16[52,128,128]{2,1,0:T(8,128)(2,1)S(1)} %get-tuple-element.187), channel_id=1, source_target_pairs={{1,0},{2,1},{3,2},{5,4},{6,5},{7,6},{9,8},{10,9},{11,10},{13,12},{... | collective-permute-start | bytes 5111816 | tf_op jit(solution)/shard_map/ppermute | solution.py:1090
  877.9 45.8 %collective-permute-start.40 = (bf16[32,128,128]{2,1,0:T(8,128)(2,1)}, bf16[32,128,128]{2,1,0:T(8,128)(2,1)}, u32[]{:S(2)}, u32[]{:S(2)}) collective-permute-start(bf16[32,128,128]{2,1,0:T(8,128)(2,1)} %get-tuple-element.198), channel_id=1, source_target_pairs={{0,16},{8,24},{16,0},{24,8},{1,17},{9,25},{17,1},{25,9},{2,18},{10... | collective-permute-start | bytes 3145736 | tf_op jit(solution)/shard_map/ppermute | solution.py:950
  893.8 29.8 %collective-permute-start.42 = (bf16[32,128,128]{2,1,0:T(8,128)(2,1)}, bf16[32,128,128]{2,1,0:T(8,128)(2,1)}, u32[]{:S(2)}, u32[]{:S(2)}) collective-permute-start(bf16[32,128,128]{2,1,0:T(8,128)(2,1)} %get-tuple-element.199), channel_id=1, source_target_pairs={{0,8},{8,0},{16,24},{24,16},{1,9},{9,1},{17,25},{25,17},{2,10},{10... | collective-permute-start | bytes 3145736 | tf_op jit(solution)/shard_map/ppermute | solution.py:950
  914.5 25.1 %collective-permute-start.52 = (bf16[32,128,128]{2,1,0:T(8,128)(2,1)}, bf16[32,128,128]{2,1,0:T(8,128)(2,1)}, u32[]{:S(2)}, u32[]{:S(2)}) collective-permute-start(bf16[32,128,128]{2,1,0:T(8,128)(2,1)} %broadcast_select_fusion.4), channel_id=1, source_target_pairs={{0,1},{3,2},{4,5},{7,6},{8,9},{11,10},{12,13},{15,14},{16,17},{19,... | collective-permute-start | bytes 3145736 | tf_op jit(solution)/shard_map/ppermute | solution.py:1076
  926.2 49.8 %collective-permute-start.43 = (bf16[2,32,128,128]{3,2,1,0:T(8,128)(2,1)S(1)}, bf16[2,32,128,128]{3,2,1,0:T(8,128)(2,1)S(1)}, u32[]{:S(2)}, u32[]{:S(2)}) collective-permute-start(bf16[2,32,128,128]{3,2,1,0:T(8,128)(2,1)S(1)} %pad_maximum_fusion.5), channel_id=1, source_target_pairs={{0,16},{8,24},{16,0},{24,8},{1,17},{9,25},{17,1},{25,9},{2,18},{10... | collective-permute-start | bytes 6291464 | tf_op jit(solution)/shard_map/ppermute | solution.py:950
  927.0 49.0 %collective-permute-start.41 = (bf16[2,32,128,128]{3,2,1,0:T(8,128)(2,1)S(1)}, bf16[2,32,128,128]{3,2,1,0:T(8,128)(2,1)S(1)}, u32[]{:S(2)}, u32[]{:S(2)}) collective-permute-start(bf16[2,32,128,128]{3,2,1,0:T(8,128)(2,1)S(1)} %pad_maximum_fusion.4), channel_id=1, source_target_pairs={{0,8},{8,0},{16,24},{24,16},{1,9},{9,1},{17,25},{25,17},{2,10},{10... | collective-permute-start | bytes 6291464 | tf_op jit(solution)/shard_map/ppermute | solution.py:950
  941.2 24.0 %collective-permute-start.55 = (bf16[32,128,128]{2,1,0:T(8,128)(2,1)S(1)}, bf16[32,128,128]{2,1,0:T(8,128)(2,1)S(1)}, u32[]{:S(2)}, u32[]{:S(2)}) collective-permute-start(bf16[32,128,128]{2,1,0:T(8,128)(2,1)S(1)} %add_convert_fusion.14), channel_id=1, source_target_pairs={{2,1},{3,2},{6,5},{7,6},{10,9},{11,10},{14,13},{15,14},{18,17},{19... | collective-permute-start | bytes 3145736 | tf_op jit(solution)/shard_map/ppermute | solution.py:1083
  944.7 23.3 %collective-permute-start.53 = (bf16[32,128,128]{2,1,0:T(8,128)(2,1)S(1)}, bf16[32,128,128]{2,1,0:T(8,128)(2,1)S(1)}, u32[]{:S(2)}, u32[]{:S(2)}) collective-permute-start(bf16[32,128,128]{2,1,0:T(8,128)(2,1)S(1)} %add_convert_fusion.14), channel_id=1, source_target_pairs={{0,1},{1,2},{4,5},{5,6},{8,9},{9,10},{12,13},{13,14},{16,17},{17,1... | collective-permute-start | bytes 3145736 | tf_op jit(solution)/shard_map/ppermute | solution.py:1082
  969.1 22.4 %collective-permute-start.54 = (bf16[32,128,128]{2,1,0:T(8,128)(2,1)S(1)}, bf16[32,128,128]{2,1,0:T(8,128)(2,1)S(1)}, u32[]{:S(2)}, u32[]{:S(2)}) collective-permute-start(bf16[32,128,128]{2,1,0:T(8,128)(2,1)S(1)} %get-tuple-element.192), channel_id=1, source_target_pairs={{0,1},{1,2},{2,3},{4,5},{5,6},{6,7},{8,9},{9,10},{10,11},{12,13},{... | collective-permute-start | bytes 3145736 | tf_op jit(solution)/shard_map/ppermute | solution.py:1089
  971.1 22.7 %collective-permute-start.56 = (bf16[32,128,128]{2,1,0:T(8,128)(2,1)S(1)}, bf16[32,128,128]{2,1,0:T(8,128)(2,1)S(1)}, u32[]{:S(2)}, u32[]{:S(2)}) collective-permute-start(bf16[32,128,128]{2,1,0:T(8,128)(2,1)S(1)} %get-tuple-element.193), channel_id=1, source_target_pairs={{1,0},{2,1},{3,2},{5,4},{6,5},{7,6},{9,8},{10,9},{11,10},{13,12},{... | collective-permute-start | bytes 3145736 | tf_op jit(solution)/shard_map/ppermute | solution.py:1090
  1025.7 24.8 %collective-permute-start.59 = (bf16[16,128,128]{2,1,0:T(8,128)(2,1)S(1)}, bf16[16,128,128]{2,1,0:T(8,128)(2,1)S(1)}, u32[]{:S(2)}, u32[]{:S(2)}) collective-permute-start(bf16[16,128,128]{2,1,0:T(8,128)(2,1)S(1)} %get-tuple-element.196), channel_id=1, source_target_pairs={{0,1},{1,2},{2,3},{4,5},{5,6},{6,7},{8,9},{9,10},{10,11},{12,13},{... | collective-permute-start | bytes 1572872 | tf_op jit(solution)/shard_map/ppermute | solution.py:1089
  1027.6 22.9 %collective-permute-start.61 = (bf16[16,128,128]{2,1,0:T(8,128)(2,1)S(1)}, bf16[16,128,128]{2,1,0:T(8,128)(2,1)S(1)}, u32[]{:S(2)}, u32[]{:S(2)}) collective-permute-start(bf16[16,128,128]{2,1,0:T(8,128)(2,1)S(1)} %get-tuple-element.197), channel_id=1, source_target_pairs={{1,0},{2,1},{3,2},{5,4},{6,5},{7,6},{9,8},{10,9},{11,10},{13,12},{... | collective-permute-start | bytes 1572872 | tf_op jit(solution)/shard_map/ppermute | solution.py:1090
  (48 other events, 749.0 us)
